TPU v7x, 32 devices: a whole 2x2x4 slice. The times are simulated.
32 devices in a mesh: band: 4 (over y, x), fft: 8 (over z, core).
Axes of the slice: x: 2, y: 2, z: 4, core: 2. Of those that a mesh axis runs over, the one named last changes fastest.
Arguments:
- coeff: bfloat16 [8, 256, 256, 256], P('band', None, 'fft'), may hold values from -6 to 6
- sphere: int32 [256, 256, 256], P(None, 'fft'), may hold values from 0 to 1, as said below
- potential: float32 [256, 256, 256], P('fft'), may hold values from -2 to 0.5
- proj_values: bfloat16 [4096, 4, 128], P('fft', None, 'band'), may hold values from -0.59765625 to 0.59765625
- tile_cell: int32 [4096], P('fft'), may hold values from 0 to 16383
- tile_atom: int32 [4096], P('fft'), may hold values from 0 to 127, as said below
- tile_count: int32 [8], P('fft'), may hold values from 64 to 512, as said below
- dion: float32 [4], replicated, may hold values from 0.3 to 3
Outputs:
- hpsi: bfloat16 [8, 256, 256, 256], P('band', None, 'fft')
Inputs may be any that keep to these rules, and one draw needn't show every extreme that they name: sphere is 1 exactly where (kx * S / 256)^2 + (ky * S / 256)^2 + (kz * S / 256)^2 < R, with kx, ky, kz the frequencies freq of the three indices, S the largest of 256, 256, 256, and R drawn from S*S/32 to S*S/16 - 1; so every frequency with sphere 1 is under a quarter of its length. `tile_atom`: a slot of slab f names an atom a with a // 16 within 3 slabs of f, counted around the periodic cell. `tile_count`: one slab is full in every draw; the others hold 64 to 256 live slots.
All inputs are finite; a program needn't handle non-finite values.
Results may differ from a plain program's by a relative error of at most 0.008.
The roundings to bfloat16 on the way count: a program that leaves them out, or rounds other values in their place, can miss the bound.
Values may be sent and summed in bfloat16 or wider, within the bound.
A program may use at most 128 MiB of HBM per device.

v0:
```python
import math

import jax
import jax.numpy as jnp
from jax import lax
from jax.sharding import PartitionSpec as P

APD = 16
REACH = 3


def from_behind(value, axis, steps):
    count = lax.axis_size(axis)
    pairs = [(source, (source + steps) % count) for source in range(count)]
    return lax.ppermute(value, axis, pairs)


def cas_table(length):
    index = jnp.arange(length, dtype=jnp.int32)
    product = index[:, None] * index[None, :] % length
    angle = product.astype(jnp.float32) * (2.0 * math.pi / length)
    return ((jnp.cos(angle) + jnp.sin(angle)) * (1.0 / math.sqrt(length))).astype(jnp.bfloat16)


def frequency(index, length):
    return jnp.minimum(index, length - index)


def local(coeff, sphere, potential, proj_values, tile_cell, tile_atom, tile_count, dion):
    high = lax.Precision.HIGHEST
    orbitals, full_x, local_y, full_z = coeff.shape
    shards = lax.axis_size("fft")
    own_index = lax.axis_index("fft")
    full_y = local_y * shards
    table_x = cas_table(full_x)
    table_y = cas_table(full_y)
    table_z = cas_table(full_z)
    sphere_real = sphere.astype(jnp.float32)
    masked = (coeff.astype(jnp.float32) * sphere_real[None]).astype(jnp.bfloat16)
    row_x = frequency(jnp.arange(full_x, dtype=jnp.int32), full_x).astype(jnp.float32)
    row_y = frequency(own_index * local_y + jnp.arange(local_y, dtype=jnp.int32), full_y).astype(
        jnp.float32
    )
    row_z = frequency(jnp.arange(full_z, dtype=jnp.int32), full_z).astype(jnp.float32)
    kinetic = 2.0 * (
        (4.0 * row_x / full_x)[:, None, None] ** 2
        + (4.0 * row_y / full_y)[None, :, None] ** 2
        + (4.0 * row_z / full_z)[None, None, :] ** 2
    )
    section_one = jnp.einsum(
        "ax,oxyz->oayz", table_x, masked, preferred_element_type=jnp.float32
    ).astype(jnp.bfloat16)
    along_y = jnp.einsum(
        "by,oxyz->oxbz",
        table_y,
        lax.all_to_all(section_one, "fft", split_axis=1, concat_axis=2, tiled=True),
        preferred_element_type=jnp.float32,
    ).astype(jnp.bfloat16)
    real = jnp.dot(along_y, table_z, preferred_element_type=jnp.float32).astype(jnp.bfloat16)
    whole_proj = lax.all_gather(proj_values, "band", axis=2, tiled=True)
    flat = real.reshape(orbitals, -1, 128)
    patches = jnp.take(flat, tile_cell, axis=1)
    slots = tile_cell.shape[0]
    live = (jnp.arange(slots, dtype=jnp.int32) < tile_count[0]).astype(jnp.float32)
    partial_value = (
        jnp.einsum("otc,tpc->otp", patches, whole_proj, preferred_element_type=jnp.float32)
        * live[None, :, None]
    )
    width = (2 * REACH + 1) * APD
    home = tile_atom // APD
    local_atom = (home - own_index + REACH) % shards * APD + tile_atom % APD
    onehot = (local_atom[:, None] == jnp.arange(width, dtype=jnp.int32)[None, :]).astype(
        jnp.float32
    )
    table = jnp.einsum("otp,ta->oap", partial_value, onehot, precision=high)
    intersection = table
    for offset in range(-2 * REACH, 2 * REACH + 1):
        if offset != 0:
            arrived = from_behind(table, "fft", offset)
            first = max(0, -offset)
            last = min(2 * REACH, 2 * REACH - offset)
            intersection = intersection.at[:, first * APD : (last + 1) * APD].add(
                arrived[:, (first + offset) * APD : (last + offset + 1) * APD]
            )
    weights = intersection * dion[None, None, :]
    back = jnp.einsum("oap,ta->otp", weights, onehot, precision=high) * live[None, :, None]
    added = jnp.einsum("otp,tpc->otc", back, whole_proj.astype(jnp.float32), precision=high)
    nonlocal_part = (
        jnp.zeros(flat.shape, jnp.float32).at[:, tile_cell].add(added).reshape(real.shape)
    )
    mixed = (potential[None] * real.astype(jnp.float32) + nonlocal_part).astype(jnp.bfloat16)
    section_three = jnp.dot(mixed, table_z, preferred_element_type=jnp.float32).astype(jnp.bfloat16)
    section_four = jnp.einsum(
        "by,oxyz->oxbz", table_y, section_three, preferred_element_type=jnp.float32
    ).astype(jnp.bfloat16)
    spectrum = jnp.einsum(
        "ax,oxyz->oayz",
        table_x,
        lax.all_to_all(section_four, "fft", split_axis=2, concat_axis=1, tiled=True),
        preferred_element_type=jnp.float32,
    )
    result = sphere_real[None] * (spectrum + kinetic[None] * masked.astype(jnp.float32))
    return result.astype(jnp.bfloat16)


def solution(mesh):
    in_specs = (
        P("band", None, "fft", None),
        P(None, "fft", None),
        P("fft", None, None),
        P("fft", None, "band"),
        P("fft"),
        P("fft"),
        P("fft"),
        P(),
    )
    out_specs = P("band", None, "fft", None)
    return jax.shard_map(local, mesh=mesh, in_specs=in_specs, out_specs=out_specs, check_vma=False)
```

profile of v0, /device:TPU:1, one launch (start us, length us, event | category | flops | bytes accessed | tf_op | source)
XLA Modules:
  0.0 682.2 jit_solution(13148682923396278589)
XLA Ops:
  0.0 8.7 %convert_element_type.105 = f32[256,32,256]{2,1,0:T(8,128)} convert(s32[256,32,256]{2,1,0:T(8,128)} %param.33) | non-fusion elementwise | flops 2097152 | bytes 16777216 | tf_op jit(solution)/shard_map/convert_element_type | solution.py:38
  8.7 9.9 %copy.28 = f32[256,32,256]{0,2,1:T(8,128)} copy(f32[256,32,256]{2,1,0:T(8,128)} %convert_element_type.105) | data formatting | bytes 16777216 | tf_op jit(solution)/shard_map/convert_element_type | solution.py:38
  18.6 13.7 %copy.29 = bf16[2,256,32,256]{1,3,2,0:T(8,128)(2,1)} copy(bf16[2,256,32,256]{3,2,1,0:T(8,128)(2,1)} %param.32) | data formatting | bytes 16777216 | tf_op args[0]
  32.3 13.5 %convert_bitcast_fusion.1 = bf16[2,256,32,256]{1,3,2,0:T(8,128)(2,1)} fusion(bf16[2,256,32,256]{1,3,2,0:T(8,128)(2,1)} %copy.29, f32[256,32,256]{0,2,1:T(8,128)} %copy.28), kind=kOutput, calls=%fused_computation.17 | convolution fusion | flops 2165374976 | bytes 25165824 | tf_op jit(solution)/shard_map/ax,oxyz->oayz/dot_general | solution.py:50
  45.9 14.6 %copy.30 = bf16[2,256,32,256]{3,2,0,1:T(8,128)(2,1)} copy(bf16[2,256,32,256]{1,3,2,0:T(8,128)(2,1)} %convert_bitcast_fusion.1) | data formatting | bytes 16777216 | tf_op jit(solution)/shard_map/convert_element_type | solution.py:52
  60.5 6.5 all-to-all-start
  67.7 0.1 copy.36
  67.8 9.7 %all_gather.3 = bf16[512,4,128]{0,1,2:T(4,128)(2,1)S(1)} all-gather(bf16[512,4,32]{0,1,2:T(4,128)(2,1)S(1)} %copy.36), channel_id=1, replica_groups=mesh['band'=4,'fft'=8] {'band'}, dimensions={2}, use_global_device_ids=true | all-gather | bytes 655360 | tf_op jit(solution)/shard_map/all_gather | solution.py:60
  77.5 0.6 copy.37
  78.2 172.0 %all-to-all-done = bf16[2,256,32,256]{3,2,0,1:T(8,128)(2,1)} async-done(((bf16[2,256,32,256]{3,2,0,1:T(8,128)(2,1)}), bf16[2,256,32,256]{3,2,0,1:T(8,128)(2,1)}, u32[]{:S(2)}, u32[]{:S(2)}) %all-to-all-start) | async-done | bytes 8388640 | tf_op jit(solution)/shard_map/all_to_all | solution.py:56
  250.1 8.2 %copy.32 = bf16[2,32,8,32,256]{4,3,2,1,0:T(8,128)(2,1)} copy(bf16[2,32,8,32,256]{4,3,0,1,2:T(8,128)(2,1)} %bitcast.5) | data formatting | bytes 16777216 | tf_op jit(solution)/shard_map/all_to_all | solution.py:56
  258.4 14.6 %fusion.18 = bf16[2,32,256,256]{3,2,1,0:T(8,128)(2,1)} fusion(bf16[2,32,256,256]{3,2,1,0:T(8,128)(2,1)} %bitcast.59), kind=kOutput, calls=%fused_computation.21 | convolution fusion | flops 4305584128 | bytes 16777216 | tf_op jit(solution)/shard_map/dot_general | solution.py:59
  272.9 12.9 %reshape.424 = bf16[2,16384,128]{2,1,0:T(8,128)(2,1)} reshape(bf16[2,32,256,256]{3,2,1,0:T(8,128)(2,1)} %fusion.18) | data formatting | bytes 16777216 | tf_op jit(solution)/shard_map/reshape | solution.py:61
  285.8 16.4 %copy.35 = bf16[2,16384,128]{2,0,1:T(2,128)(2,1)} copy(bf16[2,16384,128]{2,1,0:T(8,128)(2,1)} %reshape.424) | data formatting | bytes 16777216 | tf_op jit(solution)/shard_map/reshape | solution.py:61
  302.2 4.7 gather_fusion
  306.9 3.4 fusion.21
  310.4 0.5 fusion.24
  310.9 2.3 collective-permute-start.1
  313.3 0.8 collective-permute-start.2
  314.1 1.5 collective-permute-start.3
  315.6 2.1 collective-permute-start.4
  317.6 0.7 collective-permute-start.5
  318.3 1.0 collective-permute-start.6
  319.5 1.2 collective-permute-done.5
  320.7 0.3 scatter-add.46
  321.1 0.3 scatter-add.49
  321.5 0.3 scatter-add.50
  321.9 0.3 scatter-add.51
  322.3 0.3 scatter-add.54
  322.8 0.3 scatter-add.55
  323.2 0.1 scatter-add.56
  323.4 0.1 scatter-add.59
  323.6 0.1 scatter-add.60
  324.2 0.2 fusion.37
  324.4 0.3 copy.39
  324.7 2.0 fusion.22
  326.7 6.0 broadcast_in_dim.11
  332.7 48.9 %scatter_fusion = f32[2,16384,128]{2,0,1:T(2,128)} fusion(f32[2,16384,128]{2,0,1:T(2,128)} %broadcast_in_dim.11, s32[512]{0:T(512)S(1)} %compare_select_fusion, f32[512,2,128]{2,1,0:T(2,128)S(1)} %fusion.22), kind=kCustom, calls=%fused_computation.1 | custom fusion | flops 131072 | bytes 1574912 | tf_op jit(solution)/shard_map/scatter-add | solution.py:89
  381.6 12.6 %copy.41 = f32[2,16384,128]{2,1,0:T(8,128)} copy(f32[2,16384,128]{2,0,1:T(2,128)} %scatter_fusion) | data formatting | bytes 33554432 | tf_op jit(solution)/shard_map/scatter-add | solution.py:89
  394.2 19.1 %reshape.425 = f32[2,32,256,256]{3,2,1,0:T(8,128)} reshape(f32[2,16384,128]{2,1,0:T(8,128)} %copy.41) | data formatting | bytes 33554432 | tf_op jit(solution)/shard_map/reshape | solution.py:89
  413.3 17.8 %convert_bitcast_fusion = bf16[2,32,256,256]{2,3,1,0:T(8,128)(2,1)} fusion(f32[2,32,256,256]{3,2,1,0:T(8,128)} %reshape.425, bf16[2,32,256,256]{3,2,1,0:T(8,128)(2,1)} %fusion.18, f32[32,256,256]{2,1,0:T(8,128)} %param.34), kind=kOutput, calls=%fused_computation.13 | convolution fusion | flops 4322361344 | bytes 41943040 | tf_op jit(solution)/shard_map/by,oxyz->oxbz/dot_general | solution.py:93
  431.1 14.7 %copy.43 = bf16[2,32,256,256]{3,1,0,2:T(8,128)(2,1)} copy(bf16[2,32,256,256]{2,3,1,0:T(8,128)(2,1)} %convert_bitcast_fusion) | data formatting | bytes 16777216 | tf_op jit(solution)/shard_map/convert_element_type | solution.py:95
  445.8 7.8 %all-to-all-start.1 = ((bf16[2,32,256,256]{3,1,0,2:T(8,128)(2,1)}), bf16[2,32,256,256]{3,1,0,2:T(8,128)(2,1)}, u32[]{:S(2)}, u32[]{:S(2)}) async-start(bf16[2,32,256,256]{3,1,0,2:T(8,128)(2,1)} %copy.43), calls=%async_computation.1 | async-start | bytes 16777216 | tf_op jit(solution)/shard_map/all_to_all | solution.py:99
  453.7 4.4 add_multiply_fusion
  458.1 178.5 %all-to-all-done.1 = bf16[2,32,256,256]{3,1,0,2:T(8,128)(2,1)} async-done(((bf16[2,32,256,256]{3,1,0,2:T(8,128)(2,1)}), bf16[2,32,256,256]{3,1,0,2:T(8,128)(2,1)}, u32[]{:S(2)}, u32[]{:S(2)}) %all-to-all-start.1) | async-done | bytes 8388640 | tf_op jit(solution)/shard_map/all_to_all | solution.py:99
  636.7 12.3 %copy.45 = bf16[2,8,32,32,256]{4,3,2,1,0:T(8,128)(2,1)} copy(bf16[2,8,32,32,256]{4,2,0,3,1:T(8,128)(2,1)} %bitcast.20) | data formatting | bytes 16777216 | tf_op jit(solution)/shard_map/all_to_all | solution.py:99
  649.0 18.2 %fusion.1 = bf16[2,256,32,256]{1,3,2,0:T(8,128)(2,1)} fusion(f32[256,32,256]{0,2,1:T(8,128)} %add_multiply_fusion, f32[256,32,256]{0,2,1:T(8,128)} %copy.28, bf16[2,256,32,256]{1,3,2,0:T(8,128)(2,1)} %copy.29, bf16[2,256,32,256]{3,2,1,0:T(8,128)(2,1)} %bitcast.58), kind=kOutput, calls=%fused_computation.4 | convolution fusion | flops 2182152192 | bytes 41943040 | tf_op jit(solution)/shard_map/ax,oxyz->oayz/dot_general | solution.py:96
  667.2 14.5 %copy.47 = bf16[2,256,32,256]{3,2,1,0:T(8,128)(2,1)} copy(bf16[2,256,32,256]{1,3,2,0:T(8,128)(2,1)} %fusion.1) | data formatting | bytes 16777216 | tf_op jit(solution)/shard_map/convert_element_type | solution.py:103
  (37 shorter events, 1.4 us)
Async XLA Ops:
  60.5 7.2 %copy-start = (bf16[512,4,32]{0,2,1:T(8,128)(2,1)S(1)}, bf16[512,4,32]{0,2,1:T(8,128)(2,1)}, u32[]{:S(2)}) copy-start(bf16[512,4,32]{0,2,1:T(8,128)(2,1)} %param.35) | copy-start | bytes 393220
  60.5 17.6 %copy-start.1 = (s32[512]{0:T(512)S(1)}, s32[512]{0:T(512)}, u32[]{:S(2)}) copy-start(s32[512]{0:T(512)} %param.36) | copy-start | bytes 6148
  60.5 17.6 %copy-start.2 = (s32[512]{0:T(512)S(1)}, s32[512]{0:T(512)}, u32[]{:S(2)}) copy-start(s32[512]{0:T(512)} %param.37) | copy-start | bytes 6148
  60.5 189.6 %all-to-all-start = ((bf16[2,256,32,256]{3,2,0,1:T(8,128)(2,1)}), bf16[2,256,32,256]{3,2,0,1:T(8,128)(2,1)}, u32[]{:S(2)}, u32[]{:S(2)}) async-start(bf16[2,256,32,256]{3,2,0,1:T(8,128)(2,1)} %copy.30), calls=%async_computation | async-start | bytes 16777216 | tf_op jit(solution)/shard_map/all_to_all | solution.py:56
  285.8 38.4 %copy-start.3 = (f32[4]{0:T(128)S(1)}, f32[4]{0:T(128)}, u32[]{:S(2)}) copy-start(f32[4]{0:T(128)} %param.39) | copy-start | bytes 52
  310.9 6.7 collective-permute-start
  310.9 7.4 %collective-permute-start.1 = (f32[2,112,4]{1,2,0:T(4,128)S(1)}, f32[2,112,4]{1,2,0:T(4,128)S(1)}, u32[]{:S(2)}, u32[]{:S(2)}) collective-permute-start(f32[2,112,4]{1,2,0:T(4,128)S(1)} %bitcast.61), channel_id=1, source_target_pairs={{0,3},{1,4},{2,5},{3,6},{4,7},{5,0},{6,1},{7,2},{8,11},{9,12},{10,... | collective-permute-start | bytes 10760 | tf_op jit(solution)/shard_map/ppermute | solution.py:15
  313.3 6.2 collective-permute-start.2
  314.1 5.4 collective-permute-start.3
  315.6 3.9 collective-permute-start.4
  317.6 3.0 collective-permute-start.5
  318.3 2.3 collective-permute-start.6
  445.8 190.9 %all-to-all-start.1 = ((bf16[2,32,256,256]{3,1,0,2:T(8,128)(2,1)}), bf16[2,32,256,256]{3,1,0,2:T(8,128)(2,1)}, u32[]{:S(2)}, u32[]{:S(2)}) async-start(bf16[2,32,256,256]{3,1,0,2:T(8,128)(2,1)} %copy.43), calls=%async_computation.1 | async-start | bytes 16777216 | tf_op jit(solution)/shard_map/all_to_all | solution.py:99
where the time goes:
time: 691 us; the launch traced here: 682 us
  waiting for transfers between devices  352 us (51%)
  local copies, waits for them, and re-layouts  163 us (24%)
  matrix products  70.3 us (10%)
  other arithmetic  63.1 us (9%)
  starting transfers between devices  22.7 us (3%)
  blocking collectives  9.72 us (1%)
    all_to_all x1, waiting for transfers between devices, local(): lax.all_to_all(section_four, 'fft', split_axis=2, concat_axis=1, tiled=True)  179 us
    all_to_all x1, waiting for transfers between devices, local(): lax.all_to_all(section_one, 'fft', split_axis=1, concat_axis=2, tiled=True)  172 us
    scatter-add x1, other arithmetic, local(): jnp.zeros(flat.shape, jnp.float32).at[:, tile_cell].add(added)  48.9 us
    reshape x2, local copies, waits for them, and re-layouts, local(): flat = real.reshape(orbitals, -1, 128)  29.3 us
    reshape x1, local copies, waits for them, and re-layouts, local(): jnp.zeros(flat.shape, jnp.float32).at[:, tile_cell].add(added)  19.1 us
    dot_general x1, matrix products, local(): jnp.einsum('ax,oxyz->oayz', table_x, lax.all_to_all(section_four, 'fft',...  18.2 us
    dot_general x1, matrix products, local(): jnp.einsum('by,oxyz->oxbz', table_y, section_three, preferred_element_typ...  17.8 us
    convert_element_type x1, local copies, waits for them, and re-layouts, local(): section_four = jnp.einsum('by,oxyz->oxbz', table_y, section_three, prefer...  14.7 us
  transfers between devices with their start and end apart: 9, of which 3 were waited for; matrix products, arithmetic and copies ran while one was open for 1% of the time, Pallas kernels for 0%

commit v1 on v0

--- a/solution.py
+++ b/solution.py
@@ -3,10 +3,14 @@
 import jax
 import jax.numpy as jnp
 from jax import lax
+from jax.experimental import pallas as pl
+from jax.experimental.pallas import tpu as pltpu
 from jax.sharding import PartitionSpec as P
 
 APD = 16
 REACH = 3
+MESH = pl.DeviceIdType.MESH
+VMEM_BYTES = 58 * 2**20
 
 
 def from_behind(value, axis, steps):
@@ -26,7 +30,7 @@
     return jnp.minimum(index, length - index)
 
 
-def local(coeff, sphere, potential, proj_values, tile_cell, tile_atom, tile_count, dion):
+def general(coeff, sphere, potential, proj_values, tile_cell, tile_atom, tile_count, dion):
     high = lax.Precision.HIGHEST
     orbitals, full_x, local_y, full_z = coeff.shape
     shards = lax.axis_size("fft")
@@ -103,6 +107,501 @@
     return result.astype(jnp.bfloat16)
 
 
+def remote(source, target, send_sem, recv_sem, device):
+    return pltpu.make_async_remote_copy(
+        src_ref=source,
+        dst_ref=target,
+        send_sem=send_sem,
+        recv_sem=recv_sem,
+        device_id={"fft": device},
+        device_id_type=MESH,
+    )
+
+
+def greet(device):
+    pl.semaphore_signal(
+        pltpu.get_barrier_semaphore(), inc=1, device_id={"fft": device}, device_id_type=MESH
+    )
+
+
+CHUNKS = 8
+
+
+def spread_kernel(own, out, local_sem, send_on, send_side, recv_on, recv_side):
+    me = lax.axis_index("fft")
+    chip, core = me // 2, me % 2
+    sibling = me + 1 - 2 * core
+    below = jnp.maximum(me - 2, core)
+    above = jnp.minimum(me + 2, 6 + core)
+    greet(sibling)
+
+    @pl.when(chip > 0)
+    def _():
+        greet(below)
+
+    @pl.when(chip < 3)
+    def _():
+        greet(above)
+
+    pl.semaphore_wait(pltpu.get_barrier_semaphore(), 1 + jnp.minimum(chip, 1) + jnp.minimum(3 - chip, 1))
+
+    def piece(ref, k):
+        return ref.at[k // 4, pl.ds(k % 4 * 8, 8)]
+
+    def slot(block, k):
+        return out.at[k // 4, block, pl.ds(k % 4 * 8, 8)]
+
+    for way, edge in ((0, 0), (1, 3)):
+
+        @pl.when(chip == edge)
+        def _(way=way):
+            for orbital in range(2):
+                pltpu.make_async_copy(
+                    own.at[orbital], out.at[orbital, 2 * way + core], local_sem.at[orbital]
+                ).start()
+
+    def step(k, carry):
+        for way, edge, onward in ((0, 0, above), (1, 3, below)):
+            here = slot(2 * way + core, k)
+
+            def pass_on(source, last, way=way, here=here, onward=onward):
+                if not last:
+                    remote(source, here, send_on.at[way, k], recv_on.at[way, k], onward).start()
+                remote(source, here, send_side.at[way, k], recv_side.at[way, k], sibling).start()
+
+            def arrived(way=way, here=here, onward=onward):
+                remote(here, here, send_on.at[way, k], recv_on.at[way, k], onward).wait_recv()
+
+            @pl.when(chip == edge)
+            def _(pass_on=pass_on):
+                pass_on(piece(own, k), False)
+
+            @pl.when((chip > 0) & (chip < 3))
+            def _(pass_on=pass_on, arrived=arrived, here=here):
+                arrived()
+                pass_on(here, False)
+
+            @pl.when(chip == 3 - edge)
+            def _(pass_on=pass_on, arrived=arrived, here=here):
+                arrived()
+                pass_on(here, True)
+
+        return carry
+
+    lax.fori_loop(0, CHUNKS, step, 0)
+
+    def finish(k, carry):
+        for way, edge, onward in ((0, 0, above), (1, 3, below)):
+            here = slot(2 * way + core, k)
+            there = slot(2 * way + 1 - core, k)
+            side = remote(there, there, send_side.at[way, k], recv_side.at[way, k], sibling)
+            side.wait_recv()
+            remote(here, here, send_side.at[way, k], recv_side.at[way, k], sibling).wait_send()
+
+            @pl.when(chip != 3 - edge)
+            def _(way=way, here=here, onward=onward):
+                remote(here, here, send_on.at[way, k], recv_on.at[way, k], onward).wait_send()
+
+        return carry
+
+    lax.fori_loop(0, CHUNKS, finish, 0)
+    for way, edge in ((0, 0), (1, 3)):
+
+        @pl.when(chip == edge)
+        def _(way=way):
+            for orbital in range(2):
+                pltpu.make_async_copy(
+                    own.at[orbital], out.at[orbital, 2 * way + core], local_sem.at[orbital]
+                ).wait()
+
+
+def spread(own):
+    return pl.pallas_call(
+        spread_kernel,
+        out_shape=jax.ShapeDtypeStruct((2, 4, 32, 128, 128), jnp.bfloat16),
+        in_specs=[pl.BlockSpec(memory_space=pl.ANY)],
+        out_specs=pl.BlockSpec(memory_space=pl.ANY),
+        scratch_shapes=[pltpu.SemaphoreType.DMA((2,))] + [pltpu.SemaphoreType.DMA((2, CHUNKS))] * 4,
+        compiler_params=pltpu.CompilerParams(collective_id=0, has_side_effects=True),
+        name="spread",
+    )(own)
+
+
+def total_kernel(own, scale, out, slots, send_sem, recv_sem):
+    me = lax.axis_index("fft")
+    for step in range(1, 8):
+        greet((me + step) % 8)
+    pl.semaphore_wait(pltpu.get_barrier_semaphore(), 7)
+    for step in range(1, 8):
+        remote(own, slots.at[me], send_sem.at[step], recv_sem.at[step], (me + step) % 8).start()
+    slots[me] = own[...]
+    for step in range(1, 8):
+        source = slots.at[(me + 8 - step) % 8]
+        copy = remote(own, source, send_sem.at[step], recv_sem.at[step], (me + step) % 8)
+        copy.wait_recv()
+        copy.wait_send()
+    total = slots[0]
+    for step in range(1, 8):
+        total = total + slots[step]
+    out[...] = total * scale[...]
+
+
+def total(own, scale):
+    return pl.pallas_call(
+        total_kernel,
+        out_shape=jax.ShapeDtypeStruct(own.shape, jnp.float32),
+        in_specs=[pl.BlockSpec(memory_space=pltpu.VMEM)] * 2,
+        out_specs=pl.BlockSpec(memory_space=pltpu.VMEM),
+        scratch_shapes=[
+            pltpu.VMEM((8,) + own.shape, jnp.float32),
+            pltpu.SemaphoreType.DMA((8,)),
+            pltpu.SemaphoreType.DMA((8,)),
+        ],
+        compiler_params=pltpu.CompilerParams(collective_id=1, has_side_effects=True),
+        name="total",
+    )(own, scale)
+
+
+OWNERS = (0, 1, 6, 7)
+
+
+def collect_kernel(own, out, local_sem, send_sem, recv_sem):
+    me = lax.axis_index("fft")
+    is_owner = (me < 2) | (me >= 6)
+
+    @pl.when(is_owner)
+    def _():
+        for step in range(1, 8):
+            greet((me + step) % 8)
+
+    pl.semaphore_wait(pltpu.get_barrier_semaphore(), 4 - is_owner.astype(jnp.int32))
+    rows = pl.ds(pl.multiple_of(me * 32, 32), 32)
+
+    for block, owner in enumerate(OWNERS):
+        for orbital in range(2):
+            source = own.at[orbital, block]
+            target = out.at[orbital, :, rows]
+
+            @pl.when(me != owner)
+            def _(source=source, target=target, block=block, orbital=orbital, owner=owner):
+                remote(
+                    source, target, send_sem.at[orbital, block], recv_sem.at[orbital, me], owner
+                ).start()
+
+            @pl.when(me == owner)
+            def _(source=source, target=target, orbital=orbital):
+                pltpu.make_async_copy(source, target, local_sem.at[orbital]).start()
+
+    for block, owner in enumerate(OWNERS):
+        for orbital in range(2):
+            source = own.at[orbital, block]
+            target = out.at[orbital, :, rows]
+
+            @pl.when(me != owner)
+            def _(source=source, target=target, block=block, orbital=orbital, owner=owner):
+                remote(
+                    source, target, send_sem.at[orbital, block], recv_sem.at[orbital, me], owner
+                ).wait_send()
+
+            @pl.when(me == owner)
+            def _(source=source, target=target, orbital=orbital):
+                pltpu.make_async_copy(source, target, local_sem.at[orbital]).wait()
+
+    @pl.when(is_owner)
+    def _():
+        for step in range(1, 8):
+            sender = (me + step) % 8
+            for orbital in range(2):
+                theirs = out.at[orbital, :, pl.ds(pl.multiple_of(sender * 32, 32), 32)]
+                remote(
+                    own.at[orbital, 0],
+                    theirs,
+                    send_sem.at[orbital, 0],
+                    recv_sem.at[orbital, sender],
+                    sender,
+                ).wait_recv()
+
+
+def collect(own):
+    return pl.pallas_call(
+        collect_kernel,
+        out_shape=jax.ShapeDtypeStruct((2, 32, 256, 128), jnp.bfloat16),
+        in_specs=[pl.BlockSpec(memory_space=pl.ANY)],
+        out_specs=pl.BlockSpec(memory_space=pl.ANY),
+        scratch_shapes=[
+            pltpu.SemaphoreType.DMA((2,)),
+            pltpu.SemaphoreType.DMA((2, 4)),
+            pltpu.SemaphoreType.DMA((2, 8)),
+        ],
+        compiler_params=pltpu.CompilerParams(collective_id=2, has_side_effects=True),
+        name="collect",
+    )(own)
+
+
+def matmul(left, right):
+    return jnp.dot(left, right, preferred_element_type=jnp.float32)
+
+
+def swap(value):
+    return jnp.transpose(value, (1, 0, 2))
+
+
+def grid_kernel(
+    place, count, rows, table_x, table_y, table_z, proj, atom, real, sums, first, cells, patches
+):
+    table = table_x[...]
+
+    def along_x(group, carry):
+        block, inner = group // 4, group % 4
+        found = [matmul(table, rows[0, block, inner * 8 + k]) for k in range(8)]
+        first[:, pl.ds(pl.multiple_of(group * 8, 8), 8), :] = swap(jnp.stack(found))
+        return carry
+
+    lax.fori_loop(0, 16, along_x, 0)
+
+    def plane(x, carry):
+        second = matmul(table_y[...], first[x].astype(jnp.bfloat16)).astype(jnp.bfloat16)
+        value = matmul(second, table_z[...]).astype(jnp.bfloat16)
+        real[0, x] = value
+        wide = value.astype(jnp.float32)
+        base = pl.multiple_of(x * 512, 512)
+        cells[pl.ds(base, 256), :] = wide[:, :128]
+        cells[pl.ds(base + 256, 256), :] = wide[:, 128:]
+        return carry
+
+    lax.fori_loop(0, 32, plane, 0)
+
+    def fetch(group, carry):
+        base = pl.multiple_of(group * 8, 8)
+        for k in range(8):
+            patches[pl.ds(base + k, 1), :] = cells[pl.ds(place[base + k], 1), :]
+        return carry
+
+    lax.fori_loop(0, 64, fetch, 0)
+    high = lax.Precision.HIGHEST
+    atoms = lax.broadcasted_iota(jnp.int32, (128, 512), 0)
+    slots = lax.broadcasted_iota(jnp.int32, (128, 512), 1)
+    chosen = ((atoms == atom[...]) & (slots < count[0])).astype(jnp.float32)
+    ones = jnp.ones((8, 128), jnp.float32)
+    for p in range(4):
+        product = patches[...] * proj[p].astype(jnp.float32)
+        by_atom = jnp.dot(chosen, product, precision=high, preferred_element_type=jnp.float32)
+        summed = lax.dot_general(
+            ones, by_atom, (((1,), (1,)), ((), ())), precision=high, preferred_element_type=jnp.float32
+        )
+        sums[0, p : p + 1, :] = summed[0:1]
+
+
+def whole(shape):
+    return pl.BlockSpec(shape, lambda *_: (0,) * len(shape), pipeline_mode=pl.Buffered(1))
+
+
+def to_grid(place, count, rows, table_x, table_y, table_z, proj, atom):
+    smem = pl.BlockSpec(memory_space=pltpu.SMEM)
+    return pl.pallas_call(
+        grid_kernel,
+        grid=(2,),
+        out_shape=(
+            jax.ShapeDtypeStruct((2, 32, 256, 256), jnp.bfloat16),
+            jax.ShapeDtypeStruct((2, 4, 128), jnp.float32),
+        ),
+        in_specs=[
+            smem,
+            smem,
+            pl.BlockSpec((1, 4, 32, 128, 128), lambda o: (o, 0, 0, 0, 0)),
+            whole((32, 128)),
+            whole((256, 128)),
+            whole((128, 256)),
+            whole((4, 512, 128)),
+            whole((1, 512)),
+        ],
+        out_specs=(
+            pl.BlockSpec((1, 32, 256, 256), lambda o: (o, 0, 0, 0)),
+            pl.BlockSpec((1, 4, 128), lambda o: (o, 0, 0)),
+        ),
+        scratch_shapes=[
+            pltpu.VMEM((32, 128, 128), jnp.float32),
+            pltpu.VMEM((16384, 128), jnp.float32),
+            pltpu.VMEM((512, 128), jnp.float32),
+        ],
+        compiler_params=pltpu.CompilerParams(vmem_limit_bytes=VMEM_BYTES),
+        name="to_grid",
+    )(place, count, rows, table_x, table_y, table_z, proj, atom)
+
+
+def product_kernel(
+    place, count, real, potential, weights, proj, atom, table_z, table_y, out, cells, added, fourth
+):
+    def multiply(x, carry):
+        value = potential[x] * real[0, x].astype(jnp.float32)
+        base = pl.multiple_of(x * 512, 512)
+        cells[pl.ds(base, 256), :] = value[:, :128]
+        cells[pl.ds(base + 256, 256), :] = value[:, 128:]
+        return carry
+
+    lax.fori_loop(0, 32, multiply, 0)
+    atoms = lax.broadcasted_iota(jnp.int32, (512, 128), 1)
+    slots = lax.broadcasted_iota(jnp.int32, (512, 128), 0)
+    chosen = ((atoms == atom[...]) & (slots < count[0])).astype(jnp.float32)
+    strength = jnp.concatenate([weights[0], weights[0]], axis=0)
+    back = lax.dot_general(
+        chosen,
+        strength,
+        (((1,), (1,)), ((), ())),
+        precision=lax.Precision.HIGHEST,
+        preferred_element_type=jnp.float32,
+    )
+    patch = back[:, 0:1] * proj[0].astype(jnp.float32)
+    for p in range(1, 4):
+        patch = patch + back[:, p : p + 1] * proj[p].astype(jnp.float32)
+    added[...] = patch
+
+    def store(group, carry):
+        base = pl.multiple_of(group * 8, 8)
+        for k in range(8):
+            row = pl.ds(place[base + k], 1)
+            cells[row, :] = cells[row, :] + added[pl.ds(base + k, 1), :]
+        return carry
+
+    lax.fori_loop(0, 64, store, 0)
+
+    def plane(x, carry):
+        base = pl.multiple_of(x * 512, 512)
+        low = cells[pl.ds(base, 256), :].astype(jnp.bfloat16)
+        top = cells[pl.ds(base + 256, 256), :].astype(jnp.bfloat16)
+        third = matmul(jnp.concatenate([low, top], axis=1), table_z[...]).astype(jnp.bfloat16)
+        fourth[x] = matmul(table_y[...], third)
+        return carry
+
+    lax.fori_loop(0, 32, plane, 0)
+
+    def turn(group, carry):
+        block, inner = group // 4, group % 4
+        value = fourth[:, pl.ds(pl.multiple_of(group * 8, 8), 8), :]
+        out[0, block, pl.ds(inner * 8, 8)] = swap(value).astype(jnp.bfloat16)
+        return carry
+
+    lax.fori_loop(0, 16, turn, 0)
+
+
+def from_grid(place, count, real, potential, weights, proj, atom, table_z, table_y):
+    smem = pl.BlockSpec(memory_space=pltpu.SMEM)
+    return pl.pallas_call(
+        product_kernel,
+        grid=(2,),
+        out_shape=jax.ShapeDtypeStruct((2, 4, 32, 32, 128), jnp.bfloat16),
+        in_specs=[
+            smem,
+            smem,
+            pl.BlockSpec((1, 32, 256, 256), lambda o: (o, 0, 0, 0)),
+            whole((32, 256, 256)),
+            pl.BlockSpec((1, 4, 128), lambda o: (o, 0, 0)),
+            whole((4, 512, 128)),
+            whole((512, 1)),
+            whole((256, 128)),
+            whole((128, 256)),
+        ],
+        out_specs=pl.BlockSpec((1, 4, 32, 32, 128), lambda o: (o, 0, 0, 0, 0)),
+        scratch_shapes=[
+            pltpu.VMEM((16384, 128), jnp.float32),
+            pltpu.VMEM((512, 128), jnp.float32),
+            pltpu.VMEM((32, 128, 128), jnp.float32),
+        ],
+        compiler_params=pltpu.CompilerParams(vmem_limit_bytes=VMEM_BYTES),
+        name="from_grid",
+    )(place, count, real, potential, weights, proj, atom, table_z, table_y)
+
+
+def last_kernel(index, rows, table_x, coeff, sphere, out):
+    block, orbital = pl.program_id(0), pl.program_id(1)
+    shard = index[0]
+    used = ((block < 2) | (block >= 6)) & ((shard < 2) | (shard >= 6))
+
+    @pl.when(jnp.logical_not(used))
+    def _():
+        out[...] = jnp.zeros_like(out)
+
+    def squares(start, shape, axis):
+        at = lax.broadcasted_iota(jnp.int32, shape, axis) + start
+        return (frequency(at, 256).astype(jnp.float32) * (4.0 / 256)) ** 2
+
+    @pl.when(used)
+    def _():
+        table = table_x[...]
+        for group in range(2):
+            here = slice(group * 16, group * 16 + 16)
+            found = [matmul(table, rows[orbital, group * 16 + k]) for k in range(16)]
+            spectrum = swap(jnp.stack(found))
+            kin_xy = squares(block * 32, (32, 16, 128), 0) + squares(
+                shard * 32 + group * 16, (32, 16, 128), 1
+            )
+            for half in range(2):
+                lanes = slice(half * 128, half * 128 + 128)
+                ball = sphere[:, here, lanes].astype(jnp.float32)
+                masked = coeff[0, :, here, lanes].astype(jnp.float32) * ball
+                kinetic = 2.0 * (kin_xy + squares(half * 128, (32, 16, 128), 2))
+                result = ball * (spectrum + kinetic * masked)
+                out[0, :, here, lanes] = result.astype(jnp.bfloat16)
+
+
+def last(index, rows, table_x, coeff, sphere):
+    def used_block(b):
+        return jnp.where((b >= 2) & (b < 6), 1, b)
+
+    return pl.pallas_call(
+        last_kernel,
+        grid=(8, 2),
+        out_shape=jax.ShapeDtypeStruct(coeff.shape, jnp.bfloat16),
+        in_specs=[
+            pl.BlockSpec(memory_space=pltpu.SMEM),
+            whole((2, 32, 256, 128)),
+            pl.BlockSpec((32, 256), lambda b, o: (used_block(b), 0)),
+            pl.BlockSpec((1, 32, 32, 256), lambda b, o: (o, used_block(b), 0, 0)),
+            pl.BlockSpec((32, 32, 256), lambda b, o: (used_block(b), 0, 0)),
+        ],
+        out_specs=pl.BlockSpec((1, 32, 32, 256), lambda b, o: (o, b, 0, 0)),
+        compiler_params=pltpu.CompilerParams(vmem_limit_bytes=VMEM_BYTES),
+        name="last",
+    )(index, rows, table_x, coeff, sphere)
+
+
+def used_rows(table):
+    return jnp.concatenate([table[:64], table[192:]], axis=0)
+
+
+def inner_mask(coeff, sphere):
+    masked = (coeff.astype(jnp.float32) * sphere.astype(jnp.float32)[None]).astype(jnp.bfloat16)
+    masked = jnp.concatenate([masked[:, :64], masked[:, 192:]], axis=1)
+    near = jnp.arange(128, dtype=jnp.int32) < 64
+    return jnp.where(near, masked[..., :128], masked[..., 128:])
+
+
+def line_of_chips(coeff, sphere, potential, proj_values, tile_cell, tile_atom, tile_count, dion):
+    own_index = lax.axis_index("fft")
+    table = cas_table(256)
+    part = used_rows(table)
+    own_x = lax.dynamic_slice_in_dim(table, own_index * 32, 32, 0)
+    own_x = used_rows(own_x.T).T
+    proj = lax.all_gather(proj_values, "band", axis=2, tiled=True).transpose(1, 0, 2)
+    place = tile_cell // 512 * 512 + tile_cell % 2 * 256 + tile_cell % 512 // 2
+    rows = spread(inner_mask(coeff, sphere).transpose(0, 2, 1, 3))
+    real, sums = to_grid(
+        place, tile_count, rows, own_x, part.T, part, proj, tile_atom[None, :]
+    )
+    weights = total(sums, jnp.broadcast_to(dion[None, :, None], sums.shape))
+    fourth = from_grid(
+        place, tile_count, real, potential, weights, proj, tile_atom[:, None], part.T, part
+    )
+    return last(own_index[None], collect(fourth), table, coeff, sphere)
+
+
+def local(*values):
+    coeff, slots, shards = values[0], values[4].shape[0], lax.axis_size("fft")
+    if coeff.shape == (2, 256, 32, 256) and shards == 8 and slots == 512:
+        return line_of_chips(*values)
+    return general(*values)
+
+
 def solution(mesh):
     in_specs = (
         P("band", None, "fft", None),

time: 691 us -> 506 us (0.73); the launches traced: 682 us -> 506 us
  Pallas kernels: 0 us -> 459 us
  waiting for transfers between devices: 352 us -> 0 us
  local copies, waits for them, and re-layouts: 163 us -> 12.6 us
  matrix products: 70.3 us -> 0 us
  other arithmetic: 63.1 us -> 24.2 us
  starting transfers between devices: 22.7 us -> 0 us
    pallas_call x0 -> x6, Pallas kernels: none -> 459 us  [the longest x1 291 us: spread(): pl.pallas_call(spread_kernel, out_shape=jax.ShapeDtypeStruct((2, 4, 32, 1...]
    all_to_all x2 -> x0, waiting for transfers between devices: 351 us -> none  [the longest x1 179 us: local(): lax.all_to_all(section_four, 'fft', split_axis=2, concat_axis=1, tiled=True)]
    dot_general x8 -> x0, matrix products: 70.3 us -> none  [the longest x1 18.2 us: local(): jnp.einsum('ax,oxyz->oayz', table_x, lax.all_to_all(section_four, 'fft',...]
    scatter-add x1 -> x0, other arithmetic: 48.9 us -> none  [local(): jnp.zeros(flat.shape, jnp.float32).at[:, tile_cell].add(added)]
    reshape x3 -> x0, local copies, waits for them, and re-layouts: 48.3 us -> none  [the longest x2 29.3 us: local(): flat = real.reshape(orbitals, -1, 128)]
    convert_element_type x4 -> x1, local copies, waits for them, and re-layouts: 53.7 us -> 8.39 us  [inner_mask(): sphere.astype(jnp.float32)[None]]
    all_to_all x2 -> x0, local copies, waits for them, and re-layouts: 20.5 us -> none  [the longest x1 12.3 us: local(): lax.all_to_all(section_four, 'fft', split_axis=2, concat_axis=1, tiled=True)]
    scatter-add x13 -> x0, local copies, waits for them, and re-layouts: 15.3 us -> none  [the longest x1 12.6 us: local(): jnp.zeros(flat.shape, jnp.float32).at[:, tile_cell].add(added)]
  transfers between devices with their start and end apart: 9 -> 0, of which waited for: 3 -> 0; matrix products, arithmetic and copies ran while one was open for 1% -> 0% of each run, Pallas kernels for 0% -> 0%
where the time goes in v1:
time: 506 us
  Pallas kernels  459 us (91%)
  other arithmetic  24.2 us (5%)
  local copies, waits for them, and re-layouts  12.6 us (2%)
  blocking collectives  9.2 us (2%)
    pallas_call x1, Pallas kernels, spread(): pl.pallas_call(spread_kernel, out_shape=jax.ShapeDtypeStruct((2, 4, 32, 1...  291 us
    pallas_call x1, Pallas kernels, collect(): pl.pallas_call(collect_kernel, out_shape=jax.ShapeDtypeStruct((2, 32, 256...  70.7 us
    pallas_call x1, Pallas kernels, to_grid(): pl.pallas_call(grid_kernel, grid=(2,), out_shape=(jax.ShapeDtypeStruct((2...  36.4 us
    pallas_call x1, Pallas kernels, from_grid(): pl.pallas_call(product_kernel, grid=(2,), out_shape=jax.ShapeDtypeStruct(...  35.3 us
    pallas_call x1, Pallas kernels, last(): pl.pallas_call(last_kernel, grid=(8, 2), out_shape=jax.ShapeDtypeStruct(c...  17.6 us
    convert_element_type x1, other arithmetic, inner_mask(): (coeff.astype(jnp.float32) * sphere.astype(jnp.float32)[None]).astype(jnp...  10.6 us

profile of v1, /device:TPU:1, one launch (start us, length us, event | category | flops | bytes accessed | tf_op | source)
XLA Modules:
  0.0 506.0 jit_solution(943332537322153353)
XLA Ops:
  0.0 1.1 multiply_convert_fusion.1.table_x
  1.1 0.0 copy-start
  1.1 0.1 fusion.20
  1.2 0.7 maximum_bitcast_fusion.table_x
  1.9 0.6 pad_maximum_fusion.1
  2.5 0.7 copy.24.table_y.table_z
  3.3 0.0 slice-start
  3.3 8.8 %convert_element_type.28 = f32[256,32,256]{2,1,0:T(8,128)} convert(s32[256,32,256]{2,1,0:T(8,128)} %sphere.1) | non-fusion elementwise | flops 2097152 | bytes 16777216 | tf_op jit(solution)/shard_map/convert_element_type | solution.py:573
  12.1 0.0 copy-done
  12.1 0.0 slice-start.1
  12.1 8.4 %copy.21 = f32[256,32,256]{2,0,1:T(8,128)S(1)} copy(f32[256,32,256]{2,1,0:T(8,128)} %convert_element_type.28) | data formatting | bytes 16777216 | tf_op jit(solution)/shard_map/convert_element_type | solution.py:573
  20.5 0.0 slice-done
  20.5 0.0 slice-done.1
  20.5 10.6 %multiply_convert_fusion = bf16[2,256,32,256]{3,1,2,0:T(8,128)(2,1)S(1)} fusion(bf16[2,256,32,256]{3,2,1,0:T(8,128)(2,1)S(1)} %bitcast.13, f32[256,32,256]{2,0,1:T(8,128)S(1)} %copy.21), kind=kLoop, calls=%fused_computation | loop fusion | flops 12582912 | bytes 25165824 | tf_op jit(solution)/shard_map/convert_element_type | solution.py:573
  31.1 0.6 fusion.18
  31.7 1.8 fusion.2.own
  33.5 0.0 copy-start.1
  33.5 0.0 copy-start.3
  33.5 291.1 %spread.1.rows = bf16[2,4,32,128,128]{4,3,2,1,0:T(8,128)(2,1)} custom-call(bf16[2,32,128,128]{3,2,1,0:T(8,128)(2,1)} %fusion.2.own), custom_call_target="tpu_custom_call" | custom-call | tf_op jit(solution)/shard_map/spread/pallas_call | solution.py:219
  324.6 0.0 copy-done.1
  324.6 0.1 copy.22
  324.7 9.2 %all_gather.3 = bf16[512,4,128]{0,1,2:T(4,128)(2,1)S(1)} all-gather(bf16[512,4,32]{0,1,2:T(4,128)(2,1)S(1)} %copy.22), channel_id=1, replica_groups=mesh['band'=4,'fft'=8] {'band'}, dimensions={2}, use_global_device_ids=true | all-gather | bytes 655360 | tf_op jit(solution)/shard_map/all_gather | solution.py:585
  333.9 1.2 copy.23
  335.2 0.0 copy-done.3
  335.2 0.6 fusion.11.place
  336.4 0.0 copy-start.4
  336.4 0.0 copy-start.2
  336.5 36.4 %to_grid.1 = (bf16[2,32,256,256]{3,2,1,0:T(8,128)(2,1)}, f32[2,4,128]{2,1,0:T(4,128)}) custom-call(s32[512]{0:T(512)} %fusion.11.place, s32[1]{0:T(128)S(6)} %copy.28.count, bf16[2,4,32,128,128]{4,3,2,1,0:T(8,128)(2,1)} %spread.1.rows, bf16[32,128]{1,0:T(8,128)(2,1)} %maximum_bitcast_fusion.table_x, bf16[256,128]{1,0:T(8,128)(2,1)} %copy.24.table_y.table_z, ...), custom_call_target="tpu_custom_call" | custom-call | tf_op jit(solution)/shard_map/to_grid/pallas_call | solution.py:401
  372.8 0.0 copy-done.4
  372.8 0.7 broadcast_in_dim.25.scale
  373.5 8.0 %total.1.weights = f32[2,4,128]{2,1,0:T(4,128)} custom-call(f32[2,4,128]{2,1,0:T(4,128)} %get-tuple-element.8.own, f32[2,4,128]{2,1,0:T(4,128)} %broadcast_in_dim.25.scale), custom_call_target="tpu_custom_call" | custom-call | tf_op jit(solution)/shard_map/total/pallas_call | solution.py:250
  381.5 0.0 copy-done.2
  381.5 0.9 copy.25.atom
  382.4 35.3 %from_grid.1.own = bf16[2,4,32,32,128]{4,3,2,1,0:T(8,128)(2,1)} custom-call(s32[512]{0:T(512)} %fusion.11.place, s32[1]{0:T(128)S(6)} %copy.28.count, bf16[2,32,256,256]{3,2,1,0:T(8,128)(2,1)} %get-tuple-element.7.real, f32[32,256,256]{2,1,0:T(8,128)} %potential.1, f32[2,4,128]{2,1,0:T(4,128)} %total.1.weights, bf16[4,512,128]{2,1,0:T(8,128)(2,1)} %bitcast.15, ...), custom_call_target="tpu_custom_call" | custom-call | tf_op jit(solution)/shard_map/from_grid/pallas_call | solution.py:489
  417.6 70.7 %collect.1.rows = bf16[2,32,256,128]{3,2,1,0:T(8,128)(2,1)} custom-call(bf16[2,4,32,32,128]{4,3,2,1,0:T(8,128)(2,1)} %from_grid.1.own), custom_call_target="tpu_custom_call" | custom-call | tf_op jit(solution)/shard_map/collect/pallas_call | solution.py:326
  488.4 17.6 %last.1 = bf16[2,256,32,256]{3,2,1,0:T(8,128)(2,1)} custom-call(s32[1]{0:T(128)} %bitcast.index, bf16[2,32,256,128]{3,2,1,0:T(8,128)(2,1)} %collect.1.rows, bf16[256,256]{1,0:T(8,128)(2,1)} %copy-done, bf16[2,256,32,256]{3,2,1,0:T(8,128)(2,1)} %coeff.1, s32[256,32,256]{2,1,0:T(8,128)} %sphere.1), custom_call_target="tpu_custom_call" | custom-call | tf_op jit(solution)/shard_map/last/pallas_call | solution.py:551
  (4 shorter events, 0.0 us)
Async XLA Ops:
  1.1 11.0 %copy-start = (bf16[256,256]{1,0:T(8,128)(2,1)}, bf16[256,256]{1,0:T(8,128)(2,1)S(1)}, u32[]{:S(2)}) copy-start(bf16[256,256]{1,0:T(8,128)(2,1)S(1)} %multiply_convert_fusion.1.table_x) | copy-start | bytes 393220
  3.3 17.2 %slice-start = ((s8[8388608]{0:T(1024)(128)(4,1)}), s8[4194304]{0:T(1024)(128)(4,1)S(1)}, s32[]{:S(2)}) async-start(s8[8388608]{0:T(1024)(128)(4,1)} %bitcast.12), calls=%async_computation | async-start | bytes 8388608
  12.1 8.4 %slice-start.1 = ((s8[8388608]{0:T(1024)(128)(4,1)}), s8[4194304]{0:T(1024)(128)(4,1)S(1)}, s32[]{:S(2)}) async-start(s8[8388608]{0:T(1024)(128)(4,1)} %bitcast.12), calls=%async_computation.1 | async-start | bytes 8388608
  33.5 291.1 %copy-start.1 = (bf16[512,4,32]{0,2,1:T(8,128)(2,1)S(1)}, bf16[512,4,32]{0,2,1:T(8,128)(2,1)}, u32[]{:S(2)}) copy-start(bf16[512,4,32]{0,2,1:T(8,128)(2,1)} %param.11) | copy-start | bytes 393220
  33.5 301.7 %copy-start.3 = (s32[512]{0:T(512)S(1)}, s32[512]{0:T(512)}, u32[]{:S(2)}) copy-start(s32[512]{0:T(512)} %param.12) | copy-start | bytes 6148
  336.4 36.4 %copy-start.4 = (f32[4]{0:T(128)S(1)}, f32[4]{0:T(128)}, u32[]{:S(2)}) copy-start(f32[4]{0:T(128)} %param.15) | copy-start | bytes 52
  336.4 45.1 %copy-start.2 = (s32[512]{0:T(512)S(1)}, s32[512]{0:T(512)}, u32[]{:S(2)}) copy-start(s32[512]{0:T(512)} %param.13) | copy-start | bytes 6148

commit v2 on v1

--- a/solution.py
+++ b/solution.py
@@ -124,104 +124,128 @@
     )
 
 
-CHUNKS = 8
-
-
-def spread_kernel(own, out, local_sem, send_on, send_side, recv_on, recv_side):
+OWNERS = (0, 1, 6, 7)
+
+
+def sections_kernel(owner, coeff_low, coeff_top, sphere_low, sphere_top, table_x, out, masked):
+    @pl.when(owner[0] == 1)
+    def _():
+        near = lax.broadcasted_iota(jnp.int32, (64, 32, 128), 2) < 64
+        for half, (coeff, sphere) in enumerate(((coeff_low, sphere_low), (coeff_top, sphere_top))):
+            ball = sphere[...].astype(jnp.float32)
+            value = coeff[0].astype(jnp.float32) * ball
+            value = jnp.where(near, value[..., :128], value[..., 128:])
+            masked[:, half * 64 : half * 64 + 64, :] = swap(value).astype(jnp.bfloat16)
+
+        def along_x(block, carry):
+            planes = pl.ds(pl.multiple_of(block * 64, 64), 64)
+            table = table_x[planes, :]
+            for group in range(2):
+                found = [matmul(table, masked[group * 16 + k]) for k in range(16)]
+                value = swap(jnp.stack(found)).astype(jnp.bfloat16)
+                out[0, planes, group * 16 : group * 16 + 16, :] = value
+            return carry
+
+        lax.fori_loop(0, 4, along_x, 0)
+
+
+def sections(owner, coeff, sphere, table_x):
+    return pl.pallas_call(
+        sections_kernel,
+        grid_spec=pltpu.PrefetchScalarGridSpec(
+            num_scalar_prefetch=1,
+            grid=(2,),
+            in_specs=[
+                pl.BlockSpec((1, 64, 32, 256), lambda o, own: (o * own[0], 0, 0, 0)),
+                pl.BlockSpec((1, 64, 32, 256), lambda o, own: (o * own[0], 3, 0, 0)),
+                pl.BlockSpec((64, 32, 256), lambda o, own: (0, 0, 0)),
+                pl.BlockSpec((64, 32, 256), lambda o, own: (3, 0, 0)),
+                pl.BlockSpec((256, 128), lambda o, own: (0, 0)),
+            ],
+            out_specs=pl.BlockSpec((1, 256, 32, 128), lambda o, own: (o, 0, 0, 0)),
+            scratch_shapes=[pltpu.VMEM((32, 128, 128), jnp.bfloat16)],
+        ),
+        out_shape=jax.ShapeDtypeStruct((2, 256, 32, 128), jnp.bfloat16),
+        compiler_params=pltpu.CompilerParams(vmem_limit_bytes=VMEM_BYTES),
+        name="sections",
+    )(owner, coeff, coeff, sphere, sphere, table_x)
+
+
+def spread_kernel(own, out, local_sem, send_sem, recv_sem):
     me = lax.axis_index("fft")
-    chip, core = me // 2, me % 2
-    sibling = me + 1 - 2 * core
-    below = jnp.maximum(me - 2, core)
-    above = jnp.minimum(me + 2, 6 + core)
-    greet(sibling)
-
-    @pl.when(chip > 0)
-    def _():
-        greet(below)
-
-    @pl.when(chip < 3)
-    def _():
-        greet(above)
-
-    pl.semaphore_wait(pltpu.get_barrier_semaphore(), 1 + jnp.minimum(chip, 1) + jnp.minimum(3 - chip, 1))
-
-    def piece(ref, k):
-        return ref.at[k // 4, pl.ds(k % 4 * 8, 8)]
-
-    def slot(block, k):
-        return out.at[k // 4, block, pl.ds(k % 4 * 8, 8)]
-
-    for way, edge in ((0, 0), (1, 3)):
-
-        @pl.when(chip == edge)
-        def _(way=way):
+    is_owner = (me < 2) | (me >= 6)
+    block = jnp.where(me < 2, me, me - 4)
+
+    for owner in OWNERS:
+
+        @pl.when(me != owner)
+        def _(owner=owner):
+            greet(owner)
+
+    @pl.when(is_owner)
+    def _():
+        pl.semaphore_wait(pltpu.get_barrier_semaphore(), 7)
+
+    def planes(device):
+        return pl.ds(pl.multiple_of(device * 32, 32), 32)
+
+    def slot(orbital, at):
+        return out.at[orbital, :, pl.ds(pl.multiple_of(at * 32, 32), 32)]
+
+    def outgoing(orbital, step):
+        there = (me + step) % 8
+        return remote(
+            own.at[orbital, planes(there)],
+            slot(orbital, block),
+            send_sem.at[orbital, step],
+            recv_sem.at[orbital, block],
+            there,
+        )
+
+    def kept(orbital):
+        return pltpu.make_async_copy(
+            own.at[orbital, planes(me)], slot(orbital, block), local_sem.at[orbital]
+        )
+
+    @pl.when(is_owner)
+    def _():
+        for orbital in range(2):
+            for step in range(1, 8):
+                outgoing(orbital, step).start()
+            kept(orbital).start()
+
+    for at, owner in enumerate(OWNERS):
+
+        @pl.when(me != owner)
+        def _(at=at, owner=owner):
             for orbital in range(2):
-                pltpu.make_async_copy(
-                    own.at[orbital], out.at[orbital, 2 * way + core], local_sem.at[orbital]
-                ).start()
-
-    def step(k, carry):
-        for way, edge, onward in ((0, 0, above), (1, 3, below)):
-            here = slot(2 * way + core, k)
-
-            def pass_on(source, last, way=way, here=here, onward=onward):
-                if not last:
-                    remote(source, here, send_on.at[way, k], recv_on.at[way, k], onward).start()
-                remote(source, here, send_side.at[way, k], recv_side.at[way, k], sibling).start()
-
-            def arrived(way=way, here=here, onward=onward):
-                remote(here, here, send_on.at[way, k], recv_on.at[way, k], onward).wait_recv()
-
-            @pl.when(chip == edge)
-            def _(pass_on=pass_on):
-                pass_on(piece(own, k), False)
-
-            @pl.when((chip > 0) & (chip < 3))
-            def _(pass_on=pass_on, arrived=arrived, here=here):
-                arrived()
-                pass_on(here, False)
-
-            @pl.when(chip == 3 - edge)
-            def _(pass_on=pass_on, arrived=arrived, here=here):
-                arrived()
-                pass_on(here, True)
-
-        return carry
-
-    lax.fori_loop(0, CHUNKS, step, 0)
-
-    def finish(k, carry):
-        for way, edge, onward in ((0, 0, above), (1, 3, below)):
-            here = slot(2 * way + core, k)
-            there = slot(2 * way + 1 - core, k)
-            side = remote(there, there, send_side.at[way, k], recv_side.at[way, k], sibling)
-            side.wait_recv()
-            remote(here, here, send_side.at[way, k], recv_side.at[way, k], sibling).wait_send()
-
-            @pl.when(chip != 3 - edge)
-            def _(way=way, here=here, onward=onward):
-                remote(here, here, send_on.at[way, k], recv_on.at[way, k], onward).wait_send()
-
-        return carry
-
-    lax.fori_loop(0, CHUNKS, finish, 0)
-    for way, edge in ((0, 0), (1, 3)):
-
-        @pl.when(chip == edge)
-        def _(way=way):
-            for orbital in range(2):
-                pltpu.make_async_copy(
-                    own.at[orbital], out.at[orbital, 2 * way + core], local_sem.at[orbital]
-                ).wait()
+                remote(
+                    own.at[orbital, planes(0)],
+                    slot(orbital, at),
+                    send_sem.at[orbital, 0],
+                    recv_sem.at[orbital, at],
+                    owner,
+                ).wait_recv()
+
+    @pl.when(is_owner)
+    def _():
+        for orbital in range(2):
+            for step in range(1, 8):
+                outgoing(orbital, step).wait_send()
+            kept(orbital).wait()
 
 
 def spread(own):
     return pl.pallas_call(
         spread_kernel,
-        out_shape=jax.ShapeDtypeStruct((2, 4, 32, 128, 128), jnp.bfloat16),
+        out_shape=jax.ShapeDtypeStruct((2, 32, 128, 128), jnp.bfloat16),
         in_specs=[pl.BlockSpec(memory_space=pl.ANY)],
         out_specs=pl.BlockSpec(memory_space=pl.ANY),
-        scratch_shapes=[pltpu.SemaphoreType.DMA((2,))] + [pltpu.SemaphoreType.DMA((2, CHUNKS))] * 4,
+        scratch_shapes=[
+            pltpu.SemaphoreType.DMA((2,)),
+            pltpu.SemaphoreType.DMA((2, 8)),
+            pltpu.SemaphoreType.DMA((2, 4)),
+        ],
         compiler_params=pltpu.CompilerParams(collective_id=0, has_side_effects=True),
         name="spread",
     )(own)
@@ -262,9 +286,6 @@
     )(own, scale)
 
 
-OWNERS = (0, 1, 6, 7)
-
-
 def collect_kernel(own, out, local_sem, send_sem, recv_sem):
     me = lax.axis_index("fft")
     is_owner = (me < 2) | (me >= 6)
@@ -347,20 +368,10 @@
 
 
 def grid_kernel(
-    place, count, rows, table_x, table_y, table_z, proj, atom, real, sums, first, cells, patches
+    place, count, rows, table_y, table_z, proj, atom, real, sums, cells, patches
 ):
-    table = table_x[...]
-
-    def along_x(group, carry):
-        block, inner = group // 4, group % 4
-        found = [matmul(table, rows[0, block, inner * 8 + k]) for k in range(8)]
-        first[:, pl.ds(pl.multiple_of(group * 8, 8), 8), :] = swap(jnp.stack(found))
-        return carry
-
-    lax.fori_loop(0, 16, along_x, 0)
-
     def plane(x, carry):
-        second = matmul(table_y[...], first[x].astype(jnp.bfloat16)).astype(jnp.bfloat16)
+        second = matmul(table_y[...], rows[0, x]).astype(jnp.bfloat16)
         value = matmul(second, table_z[...]).astype(jnp.bfloat16)
         real[0, x] = value
         wide = value.astype(jnp.float32)
@@ -369,7 +380,7 @@
         cells[pl.ds(base + 256, 256), :] = wide[:, 128:]
         return carry
 
-    lax.fori_loop(0, 32, plane, 0)
+    lax.fori_loop(0, 32, plane, 0, unroll=4)
 
     def fetch(group, carry):
         base = pl.multiple_of(group * 8, 8)
@@ -396,7 +407,7 @@
     return pl.BlockSpec(shape, lambda *_: (0,) * len(shape), pipeline_mode=pl.Buffered(1))
 
 
-def to_grid(place, count, rows, table_x, table_y, table_z, proj, atom):
+def to_grid(place, count, rows, table_y, table_z, proj, atom):
     smem = pl.BlockSpec(memory_space=pltpu.SMEM)
     return pl.pallas_call(
         grid_kernel,
@@ -408,8 +419,7 @@
         in_specs=[
             smem,
             smem,
-            pl.BlockSpec((1, 4, 32, 128, 128), lambda o: (o, 0, 0, 0, 0)),
-            whole((32, 128)),
+            pl.BlockSpec((1, 32, 128, 128), lambda o: (o, 0, 0, 0)),
             whole((256, 128)),
             whole((128, 256)),
             whole((4, 512, 128)),
@@ -420,13 +430,12 @@
             pl.BlockSpec((1, 4, 128), lambda o: (o, 0, 0)),
         ),
         scratch_shapes=[
-            pltpu.VMEM((32, 128, 128), jnp.float32),
             pltpu.VMEM((16384, 128), jnp.float32),
             pltpu.VMEM((512, 128), jnp.float32),
         ],
         compiler_params=pltpu.CompilerParams(vmem_limit_bytes=VMEM_BYTES),
         name="to_grid",
-    )(place, count, rows, table_x, table_y, table_z, proj, atom)
+    )(place, count, rows, table_y, table_z, proj, atom)
 
 
 def product_kernel(
@@ -439,7 +448,7 @@
         cells[pl.ds(base + 256, 256), :] = value[:, 128:]
         return carry
 
-    lax.fori_loop(0, 32, multiply, 0)
+    lax.fori_loop(0, 32, multiply, 0, unroll=2)
     atoms = lax.broadcasted_iota(jnp.int32, (512, 128), 1)
     slots = lax.broadcasted_iota(jnp.int32, (512, 128), 0)
     chosen = ((atoms == atom[...]) & (slots < count[0])).astype(jnp.float32)
@@ -473,7 +482,7 @@
         fourth[x] = matmul(table_y[...], third)
         return carry
 
-    lax.fori_loop(0, 32, plane, 0)
+    lax.fori_loop(0, 32, plane, 0, unroll=4)
 
     def turn(group, carry):
         block, inner = group // 4, group % 4
@@ -569,25 +578,15 @@
     return jnp.concatenate([table[:64], table[192:]], axis=0)
 
 
-def inner_mask(coeff, sphere):
-    masked = (coeff.astype(jnp.float32) * sphere.astype(jnp.float32)[None]).astype(jnp.bfloat16)
-    masked = jnp.concatenate([masked[:, :64], masked[:, 192:]], axis=1)
-    near = jnp.arange(128, dtype=jnp.int32) < 64
-    return jnp.where(near, masked[..., :128], masked[..., 128:])
-
-
 def line_of_chips(coeff, sphere, potential, proj_values, tile_cell, tile_atom, tile_count, dion):
     own_index = lax.axis_index("fft")
     table = cas_table(256)
     part = used_rows(table)
-    own_x = lax.dynamic_slice_in_dim(table, own_index * 32, 32, 0)
-    own_x = used_rows(own_x.T).T
+    is_owner = ((own_index < 2) | (own_index >= 6)).astype(jnp.int32)[None]
     proj = lax.all_gather(proj_values, "band", axis=2, tiled=True).transpose(1, 0, 2)
     place = tile_cell // 512 * 512 + tile_cell % 2 * 256 + tile_cell % 512 // 2
-    rows = spread(inner_mask(coeff, sphere).transpose(0, 2, 1, 3))
-    real, sums = to_grid(
-        place, tile_count, rows, own_x, part.T, part, proj, tile_atom[None, :]
-    )
+    rows = spread(sections(is_owner, coeff, sphere, part.T))
+    real, sums = to_grid(place, tile_count, rows, part.T, part, proj, tile_atom[None, :])
     weights = total(sums, jnp.broadcast_to(dion[None, :, None], sums.shape))
     fourth = from_grid(
         place, tile_count, real, potential, weights, proj, tile_atom[:, None], part.T, part

time: 506 us -> 246 us (0.49)
  Pallas kernels: 459 us -> 227 us
  other arithmetic: 24.2 us -> 3.05 us
  local copies, waits for them, and re-layouts: 12.6 us -> 5.78 us
    pallas_call x1 -> x2, Pallas kernels: 291 us -> 83.9 us  [the longest x1 73.9 us: spread(): pl.pallas_call(spread_kernel, out_shape=jax.ShapeDtypeStruct((2, 32, 128,...]
    pallas_call x1, Pallas kernels: 36.4 us -> 16 us  [to_grid(): pl.pallas_call(grid_kernel, grid=(2,), out_shape=(jax.ShapeDtypeStruct((2...]
    convert_element_type x2 -> x0, other arithmetic: 19.5 us -> none  [the longest x1 10.6 us: inner_mask(): (coeff.astype(jnp.float32) * sphere.astype(jnp.float32)[None]).astype(jnp...]
    convert_element_type x1 -> x0, local copies, waits for them, and re-layouts: 8.39 us -> none  [inner_mask(): sphere.astype(jnp.float32)[None]]
    pallas_call x1, Pallas kernels: 35.3 us -> 29.2 us  [from_grid(): pl.pallas_call(product_kernel, grid=(2,), out_shape=jax.ShapeDtypeStruct(...]
where the time goes in v2:
time: 246 us
  Pallas kernels  227 us (92%)
  blocking collectives  8.85 us (4%)
  local copies, waits for them, and re-layouts  5.78 us (2%)
  other arithmetic  3.05 us (1%)
    pallas_call x1, Pallas kernels, spread(): pl.pallas_call(spread_kernel, out_shape=jax.ShapeDtypeStruct((2, 32, 128,...  73.9 us
    pallas_call x1, Pallas kernels, collect(): pl.pallas_call(collect_kernel, out_shape=jax.ShapeDtypeStruct((2, 32, 256...  72.5 us
    pallas_call x1, Pallas kernels, from_grid(): pl.pallas_call(product_kernel, grid=(2,), out_shape=jax.ShapeDtypeStruct(...  29.2 us
    pallas_call x1, Pallas kernels, last(): pl.pallas_call(last_kernel, grid=(8, 2), out_shape=jax.ShapeDtypeStruct(c...  17.6 us
    pallas_call x1, Pallas kernels, to_grid(): pl.pallas_call(grid_kernel, grid=(2,), out_shape=(jax.ShapeDtypeStruct((2...  16 us
    pallas_call x1, Pallas kernels, sections(): pl.pallas_call(sections_kernel, grid_spec=pltpu.PrefetchScalarGridSpec(nu...  10 us
    all_gather x1, blocking collectives, line_of_chips(): lax.all_gather(proj_values, 'band', axis=2, tiled=True).transpose(1, 0, 2)  8.85 us
    pallas_call x1, Pallas kernels, total(): pl.pallas_call(total_kernel, out_shape=jax.ShapeDtypeStruct(own.shape, jn...  7.88 us

profile of v2, /device:TPU:1, one launch (start us, length us, event | category | flops | bytes accessed | tf_op | source)
XLA Modules:
  0.0 245.5 jit_solution(12290107791703790616)
XLA Ops:
  0.7 1.3 fusion.8.place
  1.9 1.3 broadcast_in_dim.26.scale
  3.3 1.1 multiply_convert_fusion.table_x
  4.4 0.0 copy-start
  4.4 0.7 pad_maximum_fusion
  5.0 0.7 copy.18.table_x.table_y.table_z
  5.8 1.0 copy.19
  6.8 1.5 copy.22.atom
  8.3 8.8 %all_gather.3 = bf16[512,4,128]{0,1,2:T(4,128)(2,1)S(1)} all-gather(bf16[512,4,32]{0,1,2:T(4,128)(2,1)S(1)} %copy.19), channel_id=1, replica_groups=mesh['band'=4,'fft'=8] {'band'}, dimensions={2}, use_global_device_ids=true | all-gather | bytes 655360 | tf_op jit(solution)/shard_map/all_gather | solution.py:586
  17.2 1.2 copy.20
  18.4 10.0 %sections.1.own = bf16[2,256,32,128]{3,2,1,0:T(8,128)(2,1)} custom-call(s32[1]{0:T(128)} %bitcast.1.owner, bf16[2,256,32,256]{3,2,1,0:T(8,128)(2,1)} %coeff.1, bf16[2,256,32,256]{3,2,1,0:T(8,128)(2,1)} %coeff.1, s32[256,32,256]{2,1,0:T(8,128)} %sphere.1, s32[256,32,256]{2,1,0:T(8,128)} %sphere.1, bf16[256,128]{1,0:T(8,128)(2,1)} %copy.18.table_x.table_y.table_z), custom_call_target="tpu_custom_call" | custom-call | tf_op jit(solution)/shard_map/sections/pallas_call | solution.py:153
  28.4 0.0 copy-done
  28.4 73.9 %spread.1.rows = bf16[2,32,128,128]{3,2,1,0:T(8,128)(2,1)} custom-call(bf16[2,256,32,128]{3,2,1,0:T(8,128)(2,1)} %sections.1.own), custom_call_target="tpu_custom_call" | custom-call | tf_op jit(solution)/shard_map/spread/pallas_call | solution.py:239
  102.3 16.0 %to_grid.1 = (bf16[2,32,256,256]{3,2,1,0:T(8,128)(2,1)}, f32[2,4,128]{2,1,0:T(4,128)}) custom-call(s32[512]{0:T(512)} %fusion.8.place, s32[1]{0:T(128)S(6)} %copy.24.count, bf16[2,32,128,128]{3,2,1,0:T(8,128)(2,1)} %spread.1.rows, bf16[256,128]{1,0:T(8,128)(2,1)} %copy.18.table_x.table_y.table_z, bf16[128,256]{1,0:T(8,128)(2,1)} %get-tuple-element.11.table_z.table_y, ...), custom_call_target="tpu_custom_call" | custom-call | tf_op jit(solution)/shard_map/to_grid/pallas_call | solution.py:412
  118.4 7.9 %total.1.weights = f32[2,4,128]{2,1,0:T(4,128)} custom-call(f32[2,4,128]{2,1,0:T(4,128)} %get-tuple-element.8.own, f32[2,4,128]{2,1,0:T(4,128)} %broadcast_in_dim.26.scale), custom_call_target="tpu_custom_call" | custom-call | tf_op jit(solution)/shard_map/total/pallas_call | solution.py:274
  126.2 29.2 %from_grid.1.own = bf16[2,4,32,32,128]{4,3,2,1,0:T(8,128)(2,1)} custom-call(s32[512]{0:T(512)} %fusion.8.place, s32[1]{0:T(128)S(6)} %copy.24.count, bf16[2,32,256,256]{3,2,1,0:T(8,128)(2,1)} %get-tuple-element.7.real, f32[32,256,256]{2,1,0:T(8,128)} %potential.1, f32[2,4,128]{2,1,0:T(4,128)} %total.1.weights, bf16[4,512,128]{2,1,0:T(8,128)(2,1)} %bitcast.8, ...), custom_call_target="tpu_custom_call" | custom-call | tf_op jit(solution)/shard_map/from_grid/pallas_call | solution.py:498
  155.4 72.5 %collect.1.rows = bf16[2,32,256,128]{3,2,1,0:T(8,128)(2,1)} custom-call(bf16[2,4,32,32,128]{4,3,2,1,0:T(8,128)(2,1)} %from_grid.1.own), custom_call_target="tpu_custom_call" | custom-call | tf_op jit(solution)/shard_map/collect/pallas_call | solution.py:347
  227.9 17.6 %last.1 = bf16[2,256,32,256]{3,2,1,0:T(8,128)(2,1)} custom-call(s32[1]{0:T(128)} %bitcast.index, bf16[2,32,256,128]{3,2,1,0:T(8,128)(2,1)} %collect.1.rows, bf16[256,256]{1,0:T(8,128)(2,1)} %copy-done, bf16[2,256,32,256]{3,2,1,0:T(8,128)(2,1)} %coeff.1, s32[256,32,256]{2,1,0:T(8,128)} %sphere.1), custom_call_target="tpu_custom_call" | custom-call | tf_op jit(solution)/shard_map/last/pallas_call | solution.py:560
  (1 shorter events, 0.0 us)
Async XLA Ops:
  4.4 24.0 %copy-start = (bf16[256,256]{1,0:T(8,128)(2,1)}, bf16[256,256]{1,0:T(8,128)(2,1)S(1)}, u32[]{:S(2)}) copy-start(bf16[256,256]{1,0:T(8,128)(2,1)S(1)} %multiply_convert_fusion.table_x) | copy-start | bytes 393220

commit v3 on v0

--- a/solution.py
+++ b/solution.py
@@ -3,10 +3,14 @@
 import jax
 import jax.numpy as jnp
 from jax import lax
+from jax.experimental import pallas as pl
+from jax.experimental.pallas import tpu as pltpu
 from jax.sharding import PartitionSpec as P
 
 APD = 16
 REACH = 3
+MESH = pl.DeviceIdType.MESH
+VMEM_BYTES = 58 * 2**20
 
 
 def from_behind(value, axis, steps):
@@ -26,7 +30,7 @@
     return jnp.minimum(index, length - index)
 
 
-def local(coeff, sphere, potential, proj_values, tile_cell, tile_atom, tile_count, dion):
+def general(coeff, sphere, potential, proj_values, tile_cell, tile_atom, tile_count, dion):
     high = lax.Precision.HIGHEST
     orbitals, full_x, local_y, full_z = coeff.shape
     shards = lax.axis_size("fft")
@@ -103,6 +107,469 @@
     return result.astype(jnp.bfloat16)
 
 
+def remote(source, target, send_sem, recv_sem, device, axis="fft"):
+    return pltpu.make_async_remote_copy(
+        src_ref=source,
+        dst_ref=target,
+        send_sem=send_sem,
+        recv_sem=recv_sem,
+        device_id={axis: device},
+        device_id_type=MESH,
+    )
+
+
+def greet(device, axis="fft"):
+    pl.semaphore_signal(
+        pltpu.get_barrier_semaphore(), inc=1, device_id={axis: device}, device_id_type=MESH
+    )
+
+
+OWNERS = (0, 1, 6, 7)
+HIGH = lax.Precision.HIGHEST
+
+
+def matmul(left, right):
+    return jnp.dot(left, right, preferred_element_type=jnp.float32)
+
+
+def exact(left, right, dims=((1,), (0,))):
+    return lax.dot_general(
+        left, right, (dims, ((), ())), precision=HIGH, preferred_element_type=jnp.float32
+    )
+
+
+def swap(value):
+    return jnp.transpose(value, (1, 0, 2))
+
+
+def slab(at):
+    return pl.ds(pl.multiple_of(at * 32, 32), 32)
+
+
+def kernel(
+    cell, count, dion, cell_row, atom_row, own_proj, table_in, table_out, coeff, sphere, potential,
+    out,
+    waves, ball, field, first, rows, cells, proj_parts, proj, spots, patches, high_part, low_part,
+    planes_of, slot_atom, tables, fourth, back, gathered, ready, empty,
+    load_sem, zero_sem, out_sem, proj_send, proj_recv, first_send, first_recv, table_send, table_recv,
+    back_send, back_recv, keep_sem,
+):
+    me, band = lax.axis_index("fft"), lax.axis_index("band")
+    is_owner = (me < 2) | (me >= 6)
+    own_block = jnp.where(me < 2, me, me - 4)
+
+    def load_waves(orbital, half):
+        return pltpu.make_async_copy(
+            coeff.at[orbital, pl.ds(half * 192, 64)],
+            waves.at[orbital, pl.ds(half * 64, 64)],
+            load_sem.at[orbital, half],
+        )
+
+    def load_ball(half):
+        return pltpu.make_async_copy(
+            sphere.at[pl.ds(half * 192, 64)], ball.at[pl.ds(half * 64, 64)], load_sem.at[2, half]
+        )
+
+    load_field = pltpu.make_async_copy(potential, field, load_sem.at[3, 0])
+
+    def clear(step):
+        return pltpu.make_async_copy(
+            empty, out.at[step // 8, slab(step % 8)], zero_sem.at[step // 8, step % 8]
+        )
+
+    def cleared(act):
+        def one(step, carry):
+            at = step % 8
+
+            @pl.when(jnp.logical_not(is_owner) | ((at >= 2) & (at < 6)))
+            def _():
+                act(clear(step))
+
+            return carry
+
+        lax.fori_loop(0, 16, one, 0)
+
+    @pl.when(is_owner)
+    def _():
+        for half in range(2):
+            load_ball(half).start()
+            load_waves(0, half).start()
+        for half in range(2):
+            load_waves(1, half).start()
+
+    for step in range(1, 8):
+        greet((me + step) % 8)
+    for step in range(1, 4):
+        greet((band + step) % 4, "band")
+    pl.semaphore_wait(pltpu.get_barrier_semaphore(), 10)
+
+    def send_proj(step):
+        return remote(
+            own_proj,
+            proj_parts.at[band],
+            proj_send.at[step],
+            proj_recv.at[step],
+            (band + step) % 4,
+            "band",
+        )
+
+    for step in range(1, 4):
+        send_proj(step).start()
+
+    def slot(orbital, at):
+        return rows.at[orbital, :, slab(at)]
+
+    def send_first(orbital, step):
+        there = (me + step) % 8
+        return remote(
+            first.at[orbital, slab(there)],
+            slot(orbital, own_block),
+            first_send.at[orbital, step],
+            first_recv.at[orbital, own_block],
+            there,
+        )
+
+    def keep_first(orbital):
+        return pltpu.make_async_copy(
+            first.at[orbital, slab(me)], slot(orbital, own_block), keep_sem.at[0, orbital]
+        )
+
+    def section(orbital, carry):
+        near = lax.broadcasted_iota(jnp.int32, (64, 32, 128), 2) < 64
+        for half in range(2):
+            load_waves(orbital, half).wait()
+            part = pl.ds(half * 64, 64)
+            value = waves[orbital, part].astype(jnp.float32) * ball[part].astype(jnp.float32)
+            value = jnp.where(near, value[..., :128], value[..., 128:])
+            spots[:, part, :] = swap(value).astype(jnp.bfloat16)
+
+        def along_x(block, inner):
+            part = pl.ds(pl.multiple_of(block * 64, 64), 64)
+            table = table_in[part, :]
+            for group in range(2):
+                found = [matmul(table, spots[group * 16 + k]) for k in range(16)]
+                value = swap(jnp.stack(found)).astype(jnp.bfloat16)
+                first[orbital, part, group * 16 : group * 16 + 16, :] = value
+            return inner
+
+        lax.fori_loop(0, 4, along_x, 0)
+        for step in range(1, 8):
+            send_first(orbital, step).start()
+        keep_first(orbital).start()
+        return carry
+
+    @pl.when(is_owner)
+    def _():
+        for half in range(2):
+            load_ball(half).wait()
+        lax.fori_loop(0, 2, section, 0)
+
+    load_field.start()
+    empty[...] = jnp.zeros_like(empty)
+    cleared(lambda copy: copy.start())
+
+    cells_at = cell_row[...]
+    in_plane = (cells_at & 1) * 256 + ((cells_at & 511) >> 1)
+    at_row = lax.broadcasted_iota(jnp.int32, (512, 512), 0)
+    patches_at = (at_row == in_plane).astype(jnp.float32)
+    tables_row = patches_at.astype(jnp.bfloat16)
+    planes_row = jnp.broadcast_to((cells_at >> 9).astype(jnp.float32), (128, 512))
+    planes_of[...] = jnp.transpose(planes_row, (1, 0))
+    atoms = lax.broadcasted_iota(jnp.int32, (128, 512), 0)
+    slots = lax.broadcasted_iota(jnp.int32, (128, 512), 1)
+    chosen = ((atoms == atom_row[...]) & (slots < count[0])).astype(jnp.float32)
+    slot_atom[...] = jnp.transpose(chosen, (1, 0))
+    proj_parts[band] = own_proj[...]
+    for step in range(1, 4):
+        source = proj_parts.at[(band + 4 - step) % 4]
+        copy = remote(
+            own_proj, source, proj_send.at[step], proj_recv.at[step], (band + step) % 4, "band"
+        )
+        copy.wait_recv()
+        copy.wait_send()
+    lane_in = lax.broadcasted_iota(jnp.int32, (128, 128), 0)
+    lane_out = lax.broadcasted_iota(jnp.int32, (128, 128), 1)
+    for p in range(4):
+        whole = jnp.zeros((512, 128), jnp.float32)
+        for part in range(4):
+            wanted = (lane_in == lane_out + 32 * (p - part)) & (lane_out // 32 == part)
+            move = wanted.astype(jnp.float32).astype(jnp.bfloat16)
+            whole = whole + matmul(proj_parts[part], move)
+        proj[p] = whole
+    load_field.wait()
+
+    def send_table(orbital, step):
+        return remote(
+            tables.at[orbital, me],
+            tables.at[orbital, me],
+            table_send.at[orbital, step],
+            table_recv.at[orbital, step],
+            (me + step) % 8,
+        )
+
+    def send_back(orbital, block, owner):
+        return remote(
+            back.at[orbital, block],
+            gathered.at[orbital, :, slab(me)],
+            back_send.at[orbital, block],
+            back_recv.at[orbital, me],
+            owner,
+        )
+
+    def keep_back(orbital, block):
+        return pltpu.make_async_copy(
+            back.at[orbital, block], gathered.at[orbital, :, slab(me)], keep_sem.at[1, orbital]
+        )
+
+    def one_orbital(orbital, carry):
+        for at, owner in enumerate(OWNERS):
+
+            @pl.when(me != owner)
+            def _(at=at, owner=owner):
+                remote(
+                    first.at[orbital, slab(0)],
+                    slot(orbital, at),
+                    first_send.at[orbital, 0],
+                    first_recv.at[orbital, at],
+                    owner,
+                ).wait_recv()
+
+        @pl.when(is_owner)
+        def _():
+            keep_first(orbital).wait()
+
+        def to_plane(x, inner):
+            second = matmul(table_in[...], rows[orbital, x]).astype(jnp.bfloat16)
+            wide = matmul(second, table_out[...]).astype(jnp.bfloat16).astype(jnp.float32)
+            base = pl.multiple_of(x * 512, 512)
+            cells[pl.ds(base, 256), :] = wide[:, :128]
+            cells[pl.ds(base + 256, 256), :] = wide[:, 128:]
+            return inner
+
+        lax.fori_loop(0, 32, to_plane, 0, unroll=4)
+
+        def fetch(group, inner):
+            base = pl.multiple_of(group * 8, 8)
+            for k in range(8):
+                at = cell[base + k]
+                row = (at >> 9) * 512 + (at & 1) * 256 + ((at & 511) >> 1)
+                patches[pl.ds(base + k, 1), :] = cells[pl.ds(row, 1), :]
+            return inner
+
+        lax.fori_loop(0, 64, fetch, 0)
+        of_slot = slot_atom[...]
+        ones = jnp.ones((8, 128), jnp.float32)
+        for p in range(4):
+            by_atom = exact(chosen, patches[...] * proj[p])
+            tables[orbital, me, p : p + 1, :] = exact(ones, by_atom, ((1,), (1,)))[0:1]
+        for step in range(1, 8):
+            send_table(orbital, step).start()
+        for step in range(1, 8):
+            source = tables.at[orbital, (me + 8 - step) % 8]
+            copy = remote(
+                source,
+                source,
+                table_send.at[orbital, step],
+                table_recv.at[orbital, step],
+                (me + step) % 8,
+            )
+            copy.wait_recv()
+            copy.wait_send()
+        total = tables[orbital, 0]
+        for other in range(1, 8):
+            total = total + tables[orbital, other]
+        strength = exact(of_slot, jnp.concatenate([total, total], axis=0), ((1,), (1,)))
+        added = strength[:, 0:1] * dion[0] * proj[0]
+        for p in range(1, 4):
+            added = added + strength[:, p : p + 1] * dion[p] * proj[p]
+        top = added.astype(jnp.bfloat16).astype(jnp.float32)
+        high_part[...] = top
+        low_part[...] = added - top
+
+        def from_plane(x, inner):
+            here = planes_of[...] == x.astype(jnp.float32)
+            pieces = jnp.concatenate(
+                [
+                    jnp.where(here, high_part[...], 0.0).astype(jnp.bfloat16),
+                    jnp.where(here, low_part[...], 0.0).astype(jnp.bfloat16),
+                ],
+                axis=1,
+            )
+            spread = matmul(tables_row, pieces)
+            spread = spread[:, :128] + spread[:, 128:]
+            base = pl.multiple_of(x * 512, 512)
+            level = field[x]
+            left = level[:, :128] * cells[pl.ds(base, 256), :] + spread[:256]
+            right = level[:, 128:] * cells[pl.ds(base + 256, 256), :] + spread[256:]
+            mixed = jnp.concatenate([left.astype(jnp.bfloat16), right.astype(jnp.bfloat16)], axis=1)
+            third = matmul(mixed, table_in[...]).astype(jnp.bfloat16)
+            fourth[x] = matmul(table_out[...], third)
+            return inner
+
+        lax.fori_loop(0, 32, from_plane, 0, unroll=2)
+
+        def turn(group, inner):
+            value = fourth[:, pl.ds(pl.multiple_of(group * 8, 8), 8), :]
+            back[orbital, group // 4, pl.ds(group % 4 * 8, 8)] = swap(value).astype(jnp.bfloat16)
+            return inner
+
+        lax.fori_loop(0, 16, turn, 0)
+        for block, owner in enumerate(OWNERS):
+
+            @pl.when(me != owner)
+            def _(block=block, owner=owner):
+                send_back(orbital, block, owner).start()
+
+            @pl.when(me == owner)
+            def _(block=block):
+                keep_back(orbital, block).start()
+
+        return carry
+
+    lax.fori_loop(0, 2, one_orbital, 0)
+
+    def squares(start, shape, axis):
+        at = lax.broadcasted_iota(jnp.int32, shape, axis) + start
+        return (frequency(at, 256).astype(jnp.float32) * (4.0 / 256)) ** 2
+
+    def write(step):
+        orbital, block = step // 4, step % 4
+        at = block + block // 2 * 4
+        return pltpu.make_async_copy(
+            ready.at[step % 2], out.at[orbital, slab(at)], out_sem.at[step % 2]
+        )
+
+    def finish(step, carry):
+        orbital, block = step // 4, step % 4
+
+        @pl.when(block == 0)
+        def _():
+            for other in range(1, 8):
+                sender = (me + other) % 8
+                remote(
+                    back.at[orbital, 0],
+                    gathered.at[orbital, :, slab(sender)],
+                    back_send.at[orbital, 0],
+                    back_recv.at[orbital, sender],
+                    sender,
+                ).wait_recv()
+            keep_back(orbital, own_block).wait()
+
+        @pl.when(step >= 2)
+        def _():
+            write(step - 2).wait()
+
+        table = table_out[slab(block), :]
+        start = block * 32 + block // 2 * 128
+        for group in range(2):
+            here = slice(group * 16, group * 16 + 16)
+            found = [matmul(table, gathered[orbital, group * 16 + k]) for k in range(16)]
+            spectrum = swap(jnp.stack(found))
+            kin_xy = squares(start, (32, 16, 128), 0) + squares(
+                me * 32 + group * 16, (32, 16, 128), 1
+            )
+            for half in range(2):
+                lanes = slice(half * 128, half * 128 + 128)
+                inside = ball[slab(block), here, lanes].astype(jnp.float32)
+                masked = waves[orbital, slab(block), here, lanes].astype(jnp.float32) * inside
+                kinetic = 2.0 * (kin_xy + squares(half * 128, (32, 16, 128), 2))
+                result = inside * (spectrum + kinetic * masked)
+                ready[step % 2, :, here, lanes] = result.astype(jnp.bfloat16)
+        write(step).start()
+        return carry
+
+    @pl.when(is_owner)
+    def _():
+        lax.fori_loop(0, 8, finish, 0)
+        write(6).wait()
+        write(7).wait()
+        for orbital in range(2):
+            for step in range(1, 8):
+                send_first(orbital, step).wait_send()
+
+    for orbital in range(2):
+        for block, owner in enumerate(OWNERS):
+
+            @pl.when(me != owner)
+            def _(orbital=orbital, block=block, owner=owner):
+                send_back(orbital, block, owner).wait_send()
+
+    cleared(lambda copy: copy.wait())
+
+
+def line_of_chips(coeff, sphere, potential, proj_values, tile_cell, tile_atom, tile_count, dion):
+    table = cas_table(256)
+    table_out = jnp.concatenate([table[:64], table[192:]], axis=0)
+    smem = pl.BlockSpec(memory_space=pltpu.SMEM)
+    vmem = pl.BlockSpec(memory_space=pltpu.VMEM)
+    anywhere = pl.BlockSpec(memory_space=pl.ANY)
+    dma = pltpu.SemaphoreType.DMA
+    half, single = jnp.bfloat16, jnp.float32
+    return pl.pallas_call(
+        kernel,
+        out_shape=jax.ShapeDtypeStruct(coeff.shape, half),
+        in_specs=[smem] * 3 + [vmem] * 5 + [anywhere] * 3,
+        out_specs=anywhere,
+        scratch_shapes=[
+            pltpu.VMEM((2, 128, 32, 256), half),
+            pltpu.VMEM((128, 32, 256), jnp.int32),
+            pltpu.VMEM((32, 256, 256), single),
+            pltpu.VMEM((2, 256, 32, 128), half),
+            pltpu.VMEM((2, 32, 128, 128), half),
+            pltpu.VMEM((16384, 128), single),
+            pltpu.VMEM((4, 512, 128), half),
+            pltpu.VMEM((4, 512, 128), single),
+            pltpu.VMEM((32, 128, 128), half),
+            pltpu.VMEM((512, 128), single),
+            pltpu.VMEM((512, 128), single),
+            pltpu.VMEM((512, 128), single),
+            pltpu.VMEM((512, 128), single),
+            pltpu.VMEM((512, 128), single),
+            pltpu.VMEM((2, 8, 4, 128), single),
+            pltpu.VMEM((32, 128, 128), single),
+            pltpu.VMEM((2, 4, 32, 32, 128), half),
+            pltpu.VMEM((2, 32, 256, 128), half),
+            pltpu.VMEM((2, 32, 32, 256), half),
+            pltpu.VMEM((32, 32, 256), half),
+            dma((4, 2)),
+            dma((2, 8)),
+            dma((2,)),
+            dma((4,)),
+            dma((4,)),
+            dma((2, 8)),
+            dma((2, 4)),
+            dma((2, 8)),
+            dma((2, 8)),
+            dma((2, 4)),
+            dma((2, 8)),
+            dma((2, 2)),
+        ],
+        compiler_params=pltpu.CompilerParams(
+            collective_id=0, has_side_effects=True, vmem_limit_bytes=VMEM_BYTES
+        ),
+        name="hamiltonian",
+    )(
+        tile_cell,
+        tile_count,
+        dion,
+        tile_cell[None, :],
+        tile_atom[None, :],
+        proj_values.reshape(512, 128),
+        table_out.T,
+        table_out,
+        coeff,
+        sphere,
+        potential,
+    )
+
+
+def local(*values):
+    coeff, slots, shards = values[0], values[4].shape[0], lax.axis_size("fft")
+    if coeff.shape == (2, 256, 32, 256) and shards == 8 and slots == 512:
+        return line_of_chips(*values)
+    return general(*values)
+
+
 def solution(mesh):
     in_specs = (
         P("band", None, "fft", None),

time: 691 us -> 209 us (0.30); the launches traced: 682 us -> 209 us
  waiting for transfers between devices: 352 us -> 0 us
  Pallas kernels: 0 us -> 196 us
  local copies, waits for them, and re-layouts: 163 us -> 10.2 us
  matrix products: 70.3 us -> 0 us
  other arithmetic: 63.1 us -> 1.74 us
  starting transfers between devices: 22.7 us -> 0 us
  blocking collectives: 9.72 us -> 0 us
    all_to_all x2 -> x0, waiting for transfers between devices: 351 us -> none  [the longest x1 179 us: local(): lax.all_to_all(section_four, 'fft', split_axis=2, concat_axis=1, tiled=True)]
    pallas_call x0 -> x1, Pallas kernels: none -> 196 us  [line_of_chips(): pl.pallas_call(kernel, out_shape=jax.ShapeDtypeStruct(coeff.shape, half),...]
    dot_general x8 -> x0, matrix products: 70.3 us -> none  [the longest x1 18.2 us: local(): jnp.einsum('ax,oxyz->oayz', table_x, lax.all_to_all(section_four, 'fft',...]
    convert_element_type x4 -> x0, local copies, waits for them, and re-layouts: 53.7 us -> none  [the longest x1 14.7 us: local(): section_four = jnp.einsum('by,oxyz->oxbz', table_y, section_three, prefer...]
    scatter-add x1 -> x0, other arithmetic: 48.9 us -> none  [local(): jnp.zeros(flat.shape, jnp.float32).at[:, tile_cell].add(added)]
    reshape x3 -> x1, local copies, waits for them, and re-layouts: 48.3 us -> 1.66 us  [line_of_chips(): proj_values.reshape(512, 128)]
    all_to_all x2 -> x0, local copies, waits for them, and re-layouts: 20.5 us -> none  [the longest x1 12.3 us: local(): lax.all_to_all(section_four, 'fft', split_axis=2, concat_axis=1, tiled=True)]
    scatter-add x13 -> x0, local copies, waits for them, and re-layouts: 15.3 us -> none  [the longest x1 12.6 us: local(): jnp.zeros(flat.shape, jnp.float32).at[:, tile_cell].add(added)]
  transfers between devices with their start and end apart: 9 -> 0, of which waited for: 3 -> 0; matrix products, arithmetic and copies ran while one was open for 1% -> 0% of each run, Pallas kernels for 0% -> 0%
where the time goes in v3:
time: 209 us
  Pallas kernels  196 us (94%)
  local copies, waits for them, and re-layouts  10.2 us (5%)
    pallas_call x1, Pallas kernels, line_of_chips(): pl.pallas_call(kernel, out_shape=jax.ShapeDtypeStruct(coeff.shape, half),...  196 us
    unnamed x1, local copies, waits for them, and re-layouts  7.76 us

profile of v3, /device:TPU:1, one launch (start us, length us, event | category | flops | bytes accessed | tf_op | source)
XLA Modules:
  0.0 208.6 jit_solution(14562322936372439041)
XLA Ops:
  0.7 1.7 copy.11.own_proj
  2.3 1.1 multiply_convert_fusion
  3.4 0.6 pad_maximum_fusion
  4.1 0.7 copy.12.table_in
  4.8 196.0 %hamiltonian.1 = bf16[2,256,32,256]{3,2,1,0:T(8,128)(2,1)} custom-call(s32[512]{0:T(512)} %cell.1, s32[1]{0:T(128)S(6)} %copy.14.count, f32[4]{0:T(128)} %dion.1, s32[1,512]{1,0:T(1,128)} %bitcast.6, s32[1,512]{1,0:T(1,128)} %bitcast.7, bf16[512,128]{1,0:T(8,128)(2,1)} %copy.11.own_proj, bf16[256,128]{1,0:T(8,128)(2,1)} %copy.12.table_in, ...), custom_call_target="tpu_custom_call" | custom-call | tf_op jit(solution)/shard_map/hamiltonian/pallas_call | solution.py:508
  200.8 7.8 %copy.15 = bf16[2,256,32,256]{3,2,1,0:T(8,128)(2,1)} copy(bf16[2,256,32,256]{3,2,1,0:T(8,128)(2,1)} %hamiltonian.1) | data formatting | bytes 16777216
  (1 shorter events, 0.0 us)

commit v4 on v3

--- a/solution.py
+++ b/solution.py
@@ -150,8 +150,8 @@
     cell, count, dion, cell_row, atom_row, own_proj, table_in, table_out, coeff, sphere, potential,
     out,
     waves, ball, field, first, rows, cells, proj_parts, proj, spots, patches, high_part, low_part,
-    planes_of, slot_atom, tables, fourth, back, gathered, ready, empty,
-    load_sem, zero_sem, out_sem, proj_send, proj_recv, first_send, first_recv, table_send, table_recv,
+    planes_of, slot_atom, tables, fourth, back, gathered, ready, inside, kinetic,
+    load_sem, out_sem, proj_send, proj_recv, first_send, first_recv, table_send, table_recv,
     back_send, back_recv, keep_sem,
 ):
     me, band = lax.axis_index("fft"), lax.axis_index("band")
@@ -171,23 +171,6 @@
         )
 
     load_field = pltpu.make_async_copy(potential, field, load_sem.at[3, 0])
-
-    def clear(step):
-        return pltpu.make_async_copy(
-            empty, out.at[step // 8, slab(step % 8)], zero_sem.at[step // 8, step % 8]
-        )
-
-    def cleared(act):
-        def one(step, carry):
-            at = step % 8
-
-            @pl.when(jnp.logical_not(is_owner) | ((at >= 2) & (at < 6)))
-            def _():
-                act(clear(step))
-
-            return carry
-
-        lax.fori_loop(0, 16, one, 0)
 
     @pl.when(is_owner)
     def _():
@@ -253,9 +236,13 @@
             return inner
 
         lax.fori_loop(0, 4, along_x, 0)
-        for step in range(1, 8):
-            send_first(orbital, step).start()
         keep_first(orbital).start()
+
+        @pl.when(orbital == 0)
+        def _():
+            for step in range(1, 8):
+                send_first(orbital, step).start()
+
         return carry
 
     @pl.when(is_owner)
@@ -265,8 +252,6 @@
         lax.fori_loop(0, 2, section, 0)
 
     load_field.start()
-    empty[...] = jnp.zeros_like(empty)
-    cleared(lambda copy: copy.start())
 
     cells_at = cell_row[...]
     in_plane = (cells_at & 1) * 256 + ((cells_at & 511) >> 1)
@@ -298,6 +283,36 @@
         proj[p] = whole
     load_field.wait()
 
+    def squares(start, shape, axis):
+        at = lax.broadcasted_iota(jnp.int32, shape, axis) + start
+        return (frequency(at, 256).astype(jnp.float32) * (4.0 / 256)) ** 2
+
+    def inner(value):
+        near = lax.broadcasted_iota(jnp.int32, value.shape[:-1] + (128,), 2) < 64
+        return jnp.where(near, value[..., :128], value[..., 128:])
+
+    def kinetic_term(block, carry):
+        lane = lax.broadcasted_iota(jnp.int32, (1, 1, 128), 2)
+        lane_freq = jnp.where(lane < 64, lane, 128 - lane).astype(jnp.float32) * (4.0 / 256)
+        energy = 2.0 * (
+            squares(block * 32 + block // 2 * 128, (32, 1, 128), 0)
+            + squares(me * 32, (1, 32, 128), 1)
+            + lane_freq**2
+        )
+        near_ball = inner(ball[slab(block)].astype(jnp.float32))
+        inside[slab(block)] = near_ball
+        for orbital in range(2):
+            masked = inner(waves[orbital, slab(block)].astype(jnp.float32)) * near_ball
+            kinetic[orbital, slab(block)] = energy * masked
+        return carry
+
+    @pl.when(is_owner)
+    def _():
+        lax.fori_loop(0, 4, kinetic_term, 0)
+        for step in range(1, 8):
+            send_first(0, step).wait_send()
+            send_first(1, step).start()
+
     def send_table(orbital, step):
         return remote(
             tables.at[orbital, me],
@@ -307,18 +322,23 @@
             (me + step) % 8,
         )
 
-    def send_back(orbital, block, owner):
+    def slots_back(orbital, device, part):
+        return gathered.at[orbital, :, pl.ds(pl.multiple_of(device * 32 + part * 16, 16), 16)]
+
+    def send_back(orbital, part, block, owner):
         return remote(
-            back.at[orbital, block],
-            gathered.at[orbital, :, slab(me)],
-            back_send.at[orbital, block],
-            back_recv.at[orbital, me],
+            back.at[orbital, part, block],
+            slots_back(orbital, me, part),
+            back_send.at[orbital, part, block],
+            back_recv.at[orbital, part, me],
             owner,
         )
 
-    def keep_back(orbital, block):
+    def keep_back(orbital, part, block):
         return pltpu.make_async_copy(
-            back.at[orbital, block], gathered.at[orbital, :, slab(me)], keep_sem.at[1, orbital]
+            back.at[orbital, part, block],
+            slots_back(orbital, me, part),
+            keep_sem.at[1 + part, orbital],
         )
 
     def one_orbital(orbital, carry):
@@ -403,40 +423,39 @@
             right = level[:, 128:] * cells[pl.ds(base + 256, 256), :] + spread[256:]
             mixed = jnp.concatenate([left.astype(jnp.bfloat16), right.astype(jnp.bfloat16)], axis=1)
             third = matmul(mixed, table_in[...]).astype(jnp.bfloat16)
-            fourth[x] = matmul(table_out[...], third)
+            fourth[x % 16] = matmul(table_out[...], third)
             return inner
 
-        lax.fori_loop(0, 32, from_plane, 0, unroll=2)
-
-        def turn(group, inner):
-            value = fourth[:, pl.ds(pl.multiple_of(group * 8, 8), 8), :]
-            back[orbital, group // 4, pl.ds(group % 4 * 8, 8)] = swap(value).astype(jnp.bfloat16)
+        def half_slab(part, inner):
+            lax.fori_loop(0, 16, lambda x, c: from_plane(part * 16 + x, c), 0, unroll=4)
+
+            def turn(group, inmost):
+                value = fourth[:, pl.ds(pl.multiple_of(group * 8, 8), 8), :]
+                value = swap(value).astype(jnp.bfloat16)
+                back[orbital, part, group // 4, pl.ds(group % 4 * 8, 8)] = value
+                return inmost
+
+            lax.fori_loop(0, 16, turn, 0, unroll=2)
+            for block, owner in enumerate(OWNERS):
+
+                @pl.when(me != owner)
+                def _(block=block, owner=owner):
+                    send_back(orbital, part, block, owner).start()
+
+                @pl.when(me == owner)
+                def _(block=block):
+                    keep_back(orbital, part, block).start()
+
             return inner
 
-        lax.fori_loop(0, 16, turn, 0)
-        for block, owner in enumerate(OWNERS):
-
-            @pl.when(me != owner)
-            def _(block=block, owner=owner):
-                send_back(orbital, block, owner).start()
-
-            @pl.when(me == owner)
-            def _(block=block):
-                keep_back(orbital, block).start()
-
+        lax.fori_loop(0, 2, half_slab, 0)
         return carry
 
     lax.fori_loop(0, 2, one_orbital, 0)
 
-    def squares(start, shape, axis):
-        at = lax.broadcasted_iota(jnp.int32, shape, axis) + start
-        return (frequency(at, 256).astype(jnp.float32) * (4.0 / 256)) ** 2
-
     def write(step):
-        orbital, block = step // 4, step % 4
-        at = block + block // 2 * 4
         return pltpu.make_async_copy(
-            ready.at[step % 2], out.at[orbital, slab(at)], out_sem.at[step % 2]
+            ready.at[step % 2], out.at[step // 4, slab(step % 4)], out_sem.at[step % 2]
         )
 
     def finish(step, carry):
@@ -444,37 +463,29 @@
 
         @pl.when(block == 0)
         def _():
-            for other in range(1, 8):
-                sender = (me + other) % 8
-                remote(
-                    back.at[orbital, 0],
-                    gathered.at[orbital, :, slab(sender)],
-                    back_send.at[orbital, 0],
-                    back_recv.at[orbital, sender],
-                    sender,
-                ).wait_recv()
-            keep_back(orbital, own_block).wait()
+            for part in range(2):
+                for other in range(1, 8):
+                    sender = (me + other) % 8
+                    remote(
+                        back.at[orbital, part, 0],
+                        slots_back(orbital, sender, part),
+                        back_send.at[orbital, part, 0],
+                        back_recv.at[orbital, part, sender],
+                        sender,
+                    ).wait_recv()
+                keep_back(orbital, part, own_block).wait()
 
         @pl.when(step >= 2)
         def _():
             write(step - 2).wait()
 
         table = table_out[slab(block), :]
-        start = block * 32 + block // 2 * 128
         for group in range(2):
             here = slice(group * 16, group * 16 + 16)
             found = [matmul(table, gathered[orbital, group * 16 + k]) for k in range(16)]
             spectrum = swap(jnp.stack(found))
-            kin_xy = squares(start, (32, 16, 128), 0) + squares(
-                me * 32 + group * 16, (32, 16, 128), 1
-            )
-            for half in range(2):
-                lanes = slice(half * 128, half * 128 + 128)
-                inside = ball[slab(block), here, lanes].astype(jnp.float32)
-                masked = waves[orbital, slab(block), here, lanes].astype(jnp.float32) * inside
-                kinetic = 2.0 * (kin_xy + squares(half * 128, (32, 16, 128), 2))
-                result = inside * (spectrum + kinetic * masked)
-                ready[step % 2, :, here, lanes] = result.astype(jnp.bfloat16)
+            result = inside[slab(block), here] * spectrum + kinetic[orbital, slab(block), here]
+            ready[step % 2, :, here] = result.astype(jnp.bfloat16)
         write(step).start()
         return carry
 
@@ -483,18 +494,46 @@
         lax.fori_loop(0, 8, finish, 0)
         write(6).wait()
         write(7).wait()
-        for orbital in range(2):
-            for step in range(1, 8):
-                send_first(orbital, step).wait_send()
+        for step in range(1, 8):
+            send_first(1, step).wait_send()
 
     for orbital in range(2):
-        for block, owner in enumerate(OWNERS):
-
-            @pl.when(me != owner)
-            def _(orbital=orbital, block=block, owner=owner):
-                send_back(orbital, block, owner).wait_send()
-
-    cleared(lambda copy: copy.wait())
+        for part in range(2):
+            for block, owner in enumerate(OWNERS):
+
+                @pl.when(me != owner)
+                def _(orbital=orbital, part=part, block=block, owner=owner):
+                    send_back(orbital, part, block, owner).wait_send()
+
+
+def pad_kernel(owner, value, out):
+    used = (owner[0] == 1) & (pl.program_id(1) % 3 == 0)
+
+    @pl.when(used)
+    def _():
+        wide = value[0].astype(jnp.float32)
+        near = lax.broadcasted_iota(jnp.int32, wide.shape, 2) < 64
+        out[0, :, :, :128] = jnp.where(near, wide, 0.0).astype(jnp.bfloat16)
+        out[0, :, :, 128:] = jnp.where(near, 0.0, wide).astype(jnp.bfloat16)
+
+    @pl.when(jnp.logical_not(used))
+    def _():
+        out[...] = jnp.zeros_like(out)
+
+
+def pad(owner, value, shape):
+    return pl.pallas_call(
+        pad_kernel,
+        grid=(2, 4),
+        out_shape=jax.ShapeDtypeStruct(shape, jnp.bfloat16),
+        in_specs=[
+            pl.BlockSpec(memory_space=pltpu.SMEM),
+            pl.BlockSpec((1, 64, 32, 128), lambda o, b: (o, b // 2, 0, 0)),
+        ],
+        out_specs=pl.BlockSpec((1, 64, 32, 256), lambda o, b: (o, b, 0, 0)),
+        compiler_params=pltpu.CompilerParams(vmem_limit_bytes=VMEM_BYTES),
+        name="pad",
+    )(owner, value)
 
 
 def line_of_chips(coeff, sphere, potential, proj_values, tile_cell, tile_atom, tile_count, dion):
@@ -505,9 +544,11 @@
     anywhere = pl.BlockSpec(memory_space=pl.ANY)
     dma = pltpu.SemaphoreType.DMA
     half, single = jnp.bfloat16, jnp.float32
-    return pl.pallas_call(
+    own_index = lax.axis_index("fft")
+    is_owner = ((own_index < 2) | (own_index >= 6)).astype(jnp.int32)[None]
+    result = pl.pallas_call(
         kernel,
-        out_shape=jax.ShapeDtypeStruct(coeff.shape, half),
+        out_shape=jax.ShapeDtypeStruct((2, 128, 32, 128), half),
         in_specs=[smem] * 3 + [vmem] * 5 + [anywhere] * 3,
         out_specs=anywhere,
         scratch_shapes=[
@@ -526,13 +567,13 @@
             pltpu.VMEM((512, 128), single),
             pltpu.VMEM((512, 128), single),
             pltpu.VMEM((2, 8, 4, 128), single),
-            pltpu.VMEM((32, 128, 128), single),
-            pltpu.VMEM((2, 4, 32, 32, 128), half),
+            pltpu.VMEM((16, 128, 128), single),
+            pltpu.VMEM((2, 2, 4, 32, 16, 128), half),
             pltpu.VMEM((2, 32, 256, 128), half),
-            pltpu.VMEM((2, 32, 32, 256), half),
-            pltpu.VMEM((32, 32, 256), half),
+            pltpu.VMEM((2, 32, 32, 128), half),
+            pltpu.VMEM((128, 32, 128), single),
+            pltpu.VMEM((2, 128, 32, 128), single),
             dma((4, 2)),
-            dma((2, 8)),
             dma((2,)),
             dma((4,)),
             dma((4,)),
@@ -540,9 +581,9 @@
             dma((2, 4)),
             dma((2, 8)),
             dma((2, 8)),
-            dma((2, 4)),
-            dma((2, 8)),
-            dma((2, 2)),
+            dma((2, 2, 4)),
+            dma((2, 2, 8)),
+            dma((3, 2)),
         ],
         compiler_params=pltpu.CompilerParams(
             collective_id=0, has_side_effects=True, vmem_limit_bytes=VMEM_BYTES
@@ -561,6 +602,7 @@
         sphere,
         potential,
     )
+    return pad(is_owner, result, coeff.shape)
 
 
 def local(*values):

time: 209 us -> 184 us (0.88)
  Pallas kernels: 196 us -> 179 us
  local copies, waits for them, and re-layouts: 10.2 us -> 2.39 us
    pallas_call x1 -> x2, Pallas kernels: 196 us -> 179 us  [the longest x1 171 us: line_of_chips(): pl.pallas_call(kernel, out_shape=jax.ShapeDtypeStruct((2, 128, 32, 128),...]
    unnamed x1 -> x0, local copies, waits for them, and re-layouts: 7.76 us -> none
where the time goes in v4:
time: 184 us
  Pallas kernels  179 us (97%)
  local copies, waits for them, and re-layouts  2.39 us (1%)
    pallas_call x1, Pallas kernels, line_of_chips(): pl.pallas_call(kernel, out_shape=jax.ShapeDtypeStruct((2, 128, 32, 128),...  171 us
    pallas_call x1, Pallas kernels, pad(): pl.pallas_call(pad_kernel, grid=(2, 4), out_shape=jax.ShapeDtypeStruct(sh...  7.33 us

profile of v4, /device:TPU:1, one launch (start us, length us, event | category | flops | bytes accessed | tf_op | source)
XLA Modules:
  0.0 183.6 jit_solution(439072413355298290)
XLA Ops:
  0.7 1.7 copy.11.own_proj
  2.3 1.1 multiply_convert_fusion
  3.4 0.6 pad_maximum_fusion
  4.1 0.7 copy.12.table_in
  4.8 171.4 %hamiltonian.1.value = bf16[2,128,32,128]{3,2,1,0:T(8,128)(2,1)} custom-call(s32[512]{0:T(512)} %cell.1, s32[1]{0:T(128)S(6)} %copy.13.count, f32[4]{0:T(128)} %dion.1, s32[1,512]{1,0:T(1,128)} %bitcast.7, s32[1,512]{1,0:T(1,128)} %bitcast.8, bf16[512,128]{1,0:T(8,128)(2,1)} %copy.11.own_proj, bf16[256,128]{1,0:T(8,128)(2,1)} %copy.12.table_in, ...), custom_call_target="tpu_custom_call" | custom-call | tf_op jit(solution)/shard_map/hamiltonian/pallas_call | solution.py:549
  176.2 7.3 %pad.9 = bf16[2,256,32,256]{3,2,1,0:T(8,128)(2,1)} custom-call(s32[1]{0:T(128)} %bitcast.owner, bf16[2,128,32,128]{3,2,1,0:T(8,128)(2,1)} %hamiltonian.1.value), custom_call_target="tpu_custom_call" | custom-call | tf_op jit(solution)/shard_map/pad/pallas_call | solution.py:525
  (1 shorter events, 0.0 us)

commit v5 on v4

--- a/solution.py
+++ b/solution.py
@@ -125,6 +125,7 @@
 
 
 OWNERS = (0, 1, 6, 7)
+EARLY = 4
 HIGH = lax.Precision.HIGHEST
 
 
@@ -149,7 +150,7 @@
 def kernel(
     cell, count, dion, cell_row, atom_row, own_proj, table_in, table_out, coeff, sphere, potential,
     out,
-    waves, ball, field, first, rows, cells, proj_parts, proj, spots, patches, high_part, low_part,
+    waves, ball, field, first, rows, cells, proj_parts, proj, spots, patches, tiles,
     planes_of, slot_atom, tables, fourth, back, gathered, ready, inside, kinetic,
     load_sem, out_sem, proj_send, proj_recv, first_send, first_recv, table_send, table_recv,
     back_send, back_recv, keep_sem,
@@ -311,6 +312,7 @@
         lax.fori_loop(0, 4, kinetic_term, 0)
         for step in range(1, 8):
             send_first(0, step).wait_send()
+        for step in range(1, EARLY):
             send_first(1, step).start()
 
     def send_table(orbital, step):
@@ -384,6 +386,12 @@
             tables[orbital, me, p : p + 1, :] = exact(ones, by_atom, ((1,), (1,)))[0:1]
         for step in range(1, 8):
             send_table(orbital, step).start()
+
+        @pl.when(is_owner & (orbital == 0))
+        def _():
+            for step in range(EARLY, 8):
+                send_first(1, step).start()
+
         for step in range(1, 8):
             source = tables.at[orbital, (me + 8 - step) % 8]
             copy = remote(
@@ -402,21 +410,20 @@
         added = strength[:, 0:1] * dion[0] * proj[0]
         for p in range(1, 4):
             added = added + strength[:, p : p + 1] * dion[p] * proj[p]
-        top = added.astype(jnp.bfloat16).astype(jnp.float32)
-        high_part[...] = top
-        low_part[...] = added - top
-
-        def from_plane(x, inner):
-            here = planes_of[...] == x.astype(jnp.float32)
-            pieces = jnp.concatenate(
-                [
-                    jnp.where(here, high_part[...], 0.0).astype(jnp.bfloat16),
-                    jnp.where(here, low_part[...], 0.0).astype(jnp.bfloat16),
-                ],
-                axis=1,
-            )
-            spread = matmul(tables_row, pieces)
-            spread = spread[:, :128] + spread[:, 128:]
+        tiles[...] = added
+
+        def from_planes(pair, inner):
+            pieces = [
+                jnp.where(planes_of[...] == (2 * pair + k).astype(jnp.float32), tiles[...], 0.0)
+                for k in range(2)
+            ]
+            pieces = jnp.concatenate([piece.astype(jnp.bfloat16) for piece in pieces], axis=1)
+            both = matmul(tables_row, pieces)
+            for k in range(2):
+                from_plane(2 * pair + k, both[:, k * 128 : k * 128 + 128])
+            return inner
+
+        def from_plane(x, spread):
             base = pl.multiple_of(x * 512, 512)
             level = field[x]
             left = level[:, :128] * cells[pl.ds(base, 256), :] + spread[:256]
@@ -424,10 +431,9 @@
             mixed = jnp.concatenate([left.astype(jnp.bfloat16), right.astype(jnp.bfloat16)], axis=1)
             third = matmul(mixed, table_in[...]).astype(jnp.bfloat16)
             fourth[x % 16] = matmul(table_out[...], third)
-            return inner
 
         def half_slab(part, inner):
-            lax.fori_loop(0, 16, lambda x, c: from_plane(part * 16 + x, c), 0, unroll=4)
+            lax.fori_loop(0, 8, lambda x, c: from_planes(part * 8 + x, c), 0, unroll=2)
 
             def turn(group, inmost):
                 value = fourth[:, pl.ds(pl.multiple_of(group * 8, 8), 8), :]
@@ -561,7 +567,6 @@
             pltpu.VMEM((4, 512, 128), half),
             pltpu.VMEM((4, 512, 128), single),
             pltpu.VMEM((32, 128, 128), half),
-            pltpu.VMEM((512, 128), single),
             pltpu.VMEM((512, 128), single),
             pltpu.VMEM((512, 128), single),
             pltpu.VMEM((512, 128), single),

time: 184 us -> 165 us (0.90)
  Pallas kernels: 179 us -> 160 us
    pallas_call x1, Pallas kernels: 171 us -> 152 us  [line_of_chips(): pl.pallas_call(kernel, out_shape=jax.ShapeDtypeStruct((2, 128, 32, 128),...]
where the time goes in v5:
time: 165 us; the launch traced here: 164 us
  Pallas kernels  160 us (97%)
  local copies, waits for them, and re-layouts  2.39 us (1%)
  other arithmetic  1.73 us (1%)
    pallas_call x1, Pallas kernels, line_of_chips(): pl.pallas_call(kernel, out_shape=jax.ShapeDtypeStruct((2, 128, 32, 128),...  152 us
    pallas_call x1, Pallas kernels, pad(): pl.pallas_call(pad_kernel, grid=(2, 4), out_shape=jax.ShapeDtypeStruct(sh...  7.33 us

profile of v5, /device:TPU:1, one launch (start us, length us, event | category | flops | bytes accessed | tf_op | source)
XLA Modules:
  0.0 164.4 jit_solution(11756262731994836339)
XLA Ops:
  0.7 1.7 %copy.11.own_proj = bf16[512,128]{1,0:T(8,128)(2,1)} copy(bf16[512,128]{0,1:T(8,128)(2,1)} %bitcast.6) | data formatting | bytes 262144 | tf_op jit(solution)/shard_map/reshape | solution.py:603
  2.3 1.1 multiply_convert_fusion
  3.4 0.6 pad_maximum_fusion
  4.1 0.7 copy.12.table_in
  4.8 152.2 %hamiltonian.1.value = bf16[2,128,32,128]{3,2,1,0:T(8,128)(2,1)} custom-call(s32[512]{0:T(512)} %cell.1, s32[1]{0:T(128)S(6)} %copy.13.count, f32[4]{0:T(128)} %dion.1, s32[1,512]{1,0:T(1,128)} %bitcast.7, s32[1,512]{1,0:T(1,128)} %bitcast.8, bf16[512,128]{1,0:T(8,128)(2,1)} %copy.11.own_proj, bf16[256,128]{1,0:T(8,128)(2,1)} %copy.12.table_in, ...), custom_call_target="tpu_custom_call" | custom-call | tf_op jit(solution)/shard_map/hamiltonian/pallas_call | solution.py:555
  157.0 7.3 %pad.9 = bf16[2,256,32,256]{3,2,1,0:T(8,128)(2,1)} custom-call(s32[1]{0:T(128)} %bitcast.owner, bf16[2,128,32,128]{3,2,1,0:T(8,128)(2,1)} %hamiltonian.1.value), custom_call_target="tpu_custom_call" | custom-call | tf_op jit(solution)/shard_map/pad/pallas_call | solution.py:531
  (1 shorter events, 0.0 us)

commit v6 on v5

--- a/solution.py
+++ b/solution.py
@@ -234,16 +234,17 @@
                 found = [matmul(table, spots[group * 16 + k]) for k in range(16)]
                 value = swap(jnp.stack(found)).astype(jnp.bfloat16)
                 first[orbital, part, group * 16 : group * 16 + 16, :] = value
+            for k in range(2):
+                step = (2 * block + k + 8 - me) % 8
+
+                @pl.when((orbital == 0) & (step > 0))
+                def _(step=step):
+                    send_first(0, step).start()
+
             return inner
 
         lax.fori_loop(0, 4, along_x, 0)
         keep_first(orbital).start()
-
-        @pl.when(orbital == 0)
-        def _():
-            for step in range(1, 8):
-                send_first(orbital, step).start()
-
         return carry
 
     @pl.when(is_owner)
@@ -391,6 +392,12 @@
         def _():
             for step in range(EARLY, 8):
                 send_first(1, step).start()
+
+        for block in (1, 3):
+
+            @pl.when((orbital == 1) & (me != OWNERS[block]))
+            def _(block=block):
+                send_back(0, 1, block, OWNERS[block]).start()
 
         for step in range(1, 8):
             source = tables.at[orbital, (me + 8 - step) % 8]
@@ -444,7 +451,9 @@
             lax.fori_loop(0, 16, turn, 0, unroll=2)
             for block, owner in enumerate(OWNERS):
 
-                @pl.when(me != owner)
+                later = (orbital == 0) & (part == 1) & (block % 2 == 1)
+
+                @pl.when((me != owner) & jnp.logical_not(later))
                 def _(block=block, owner=owner):
                     send_back(orbital, part, block, owner).start()
 
@@ -512,34 +521,65 @@
                     send_back(orbital, part, block, owner).wait_send()
 
 
-def pad_kernel(owner, value, out):
-    used = (owner[0] == 1) & (pl.program_id(1) % 3 == 0)
-
-    @pl.when(used)
+def pad_kernel(value, out, empty, wide, sems):
+    me = lax.axis_index("fft")
+    is_owner = (me < 2) | (me >= 6)
+    empty[...] = jnp.zeros_like(empty)
+
+    def clear(orbital, part):
+        return pltpu.make_async_copy(
+            empty, out.at[orbital, pl.ds(part * 64, 64)], sems.at[orbital, part]
+        )
+
+    def place(orbital, half):
+        return pltpu.make_async_copy(
+            wide.at[orbital, half], out.at[orbital, pl.ds(half * 192, 64)], sems.at[orbital, half * 3]
+        )
+
+    for orbital in range(2):
+        for part in (1, 2):
+            clear(orbital, part).start()
+
+    @pl.when(jnp.logical_not(is_owner))
     def _():
-        wide = value[0].astype(jnp.float32)
-        near = lax.broadcasted_iota(jnp.int32, wide.shape, 2) < 64
-        out[0, :, :, :128] = jnp.where(near, wide, 0.0).astype(jnp.bfloat16)
-        out[0, :, :, 128:] = jnp.where(near, 0.0, wide).astype(jnp.bfloat16)
-
-    @pl.when(jnp.logical_not(used))
+        for orbital in range(2):
+            for part in (0, 3):
+                clear(orbital, part).start()
+            for part in (0, 3):
+                clear(orbital, part).wait()
+
+    @pl.when(is_owner)
     def _():
-        out[...] = jnp.zeros_like(out)
-
-
-def pad(owner, value, shape):
+        near = lax.broadcasted_iota(jnp.int32, (64, 32, 128), 2) < 64
+        for orbital in range(2):
+            for half in range(2):
+                block = value[orbital, half * 64 : half * 64 + 64].astype(jnp.float32)
+                wide[orbital, half, :, :, :128] = jnp.where(near, block, 0.0).astype(jnp.bfloat16)
+                wide[orbital, half, :, :, 128:] = jnp.where(near, 0.0, block).astype(jnp.bfloat16)
+                place(orbital, half).start()
+        for orbital in range(2):
+            for half in range(2):
+                place(orbital, half).wait()
+
+    for orbital in range(2):
+        for part in (1, 2):
+            clear(orbital, part).wait()
+
+
+def pad(value, shape):
     return pl.pallas_call(
         pad_kernel,
-        grid=(2, 4),
         out_shape=jax.ShapeDtypeStruct(shape, jnp.bfloat16),
-        in_specs=[
-            pl.BlockSpec(memory_space=pltpu.SMEM),
-            pl.BlockSpec((1, 64, 32, 128), lambda o, b: (o, b // 2, 0, 0)),
+        in_specs=[pl.BlockSpec(memory_space=pltpu.VMEM)],
+        out_specs=pl.BlockSpec(memory_space=pl.ANY),
+        scratch_shapes=[
+            pltpu.VMEM((64, 32, 256), jnp.bfloat16),
+            pltpu.VMEM((2, 2, 64, 32, 256), jnp.bfloat16),
+            pltpu.SemaphoreType.DMA((2, 4)),
         ],
-        out_specs=pl.BlockSpec((1, 64, 32, 256), lambda o, b: (o, b, 0, 0)),
         compiler_params=pltpu.CompilerParams(vmem_limit_bytes=VMEM_BYTES),
         name="pad",
-    )(owner, value)
+    )(value)
 
 
 def line_of_chips(coeff, sphere, potential, proj_values, tile_cell, tile_atom, tile_count, dion):
@@ -550,8 +590,6 @@
     anywhere = pl.BlockSpec(memory_space=pl.ANY)
     dma = pltpu.SemaphoreType.DMA
     half, single = jnp.bfloat16, jnp.float32
-    own_index = lax.axis_index("fft")
-    is_owner = ((own_index < 2) | (own_index >= 6)).astype(jnp.int32)[None]
     result = pl.pallas_call(
         kernel,
         out_shape=jax.ShapeDtypeStruct((2, 128, 32, 128), half),
@@ -607,7 +645,7 @@
         sphere,
         potential,
     )
-    return pad(is_owner, result, coeff.shape)
+    return pad(result, coeff.shape)
 
 
 def local(*values):

time: 165 us -> 172 us (1.042)
  Pallas kernels: 160 us -> 167 us
    pallas_call x1, Pallas kernels: 152 us -> 162 us  [line_of_chips(): pl.pallas_call(kernel, out_shape=jax.ShapeDtypeStruct((2, 128, 32, 128),...]
    pallas_call x1, Pallas kernels: 7.33 us -> 5.03 us  [pad(): pl.pallas_call(pad_kernel, out_shape=jax.ShapeDtypeStruct(shape, jnp.bflo...]
where the time goes in v6:
time: 172 us; the launch traced here: 171 us
  Pallas kernels  167 us (97%)
  local copies, waits for them, and re-layouts  2.39 us (1%)
  other arithmetic  1.73 us (1%)
    pallas_call x1, Pallas kernels, line_of_chips(): pl.pallas_call(kernel, out_shape=jax.ShapeDtypeStruct((2, 128, 32, 128),...  162 us
    pallas_call x1, Pallas kernels, pad(): pl.pallas_call(pad_kernel, out_shape=jax.ShapeDtypeStruct(shape, jnp.bflo...  5.03 us

profile of v6, /device:TPU:1, one launch (start us, length us, event | category | flops | bytes accessed | tf_op | source)
XLA Modules:
  0.0 171.3 jit_solution(1375742113816902892)
XLA Ops:
  0.7 1.7 copy.11.own_proj
  2.3 1.1 multiply_convert_fusion
  3.4 0.6 pad_maximum_fusion
  4.1 0.7 copy.12.table_in
  4.8 161.5 %hamiltonian.1.value = bf16[2,128,32,128]{3,2,1,0:T(8,128)(2,1)} custom-call(s32[512]{0:T(512)} %cell.1, s32[1]{0:T(128)S(6)} %copy.13.count, f32[4]{0:T(128)} %dion.1, s32[1,512]{1,0:T(1,128)} %bitcast.6, s32[1,512]{1,0:T(1,128)} %bitcast.7, bf16[512,128]{1,0:T(8,128)(2,1)} %copy.11.own_proj, bf16[256,128]{1,0:T(8,128)(2,1)} %copy.12.table_in, ...), custom_call_target="tpu_custom_call" | custom-call | tf_op jit(solution)/shard_map/hamiltonian/pallas_call | solution.py:593
  166.3 5.0 %pad.9 = bf16[2,256,32,256]{3,2,1,0:T(8,128)(2,1)} custom-call(bf16[2,128,32,128]{3,2,1,0:T(8,128)(2,1)} %hamiltonian.1.value), custom_call_target="tpu_custom_call" | custom-call | tf_op jit(solution)/shard_map/pad/pallas_call | solution.py:570
  (1 shorter events, 0.0 us)

commit v7 on v6

--- a/solution.py
+++ b/solution.py
@@ -234,17 +234,16 @@
                 found = [matmul(table, spots[group * 16 + k]) for k in range(16)]
                 value = swap(jnp.stack(found)).astype(jnp.bfloat16)
                 first[orbital, part, group * 16 : group * 16 + 16, :] = value
-            for k in range(2):
-                step = (2 * block + k + 8 - me) % 8
-
-                @pl.when((orbital == 0) & (step > 0))
-                def _(step=step):
-                    send_first(0, step).start()
-
             return inner
 
         lax.fori_loop(0, 4, along_x, 0)
         keep_first(orbital).start()
+
+        @pl.when(orbital == 0)
+        def _():
+            for step in range(1, 8):
+                send_first(orbital, step).start()
+
         return carry
 
     @pl.when(is_owner)
@@ -392,12 +391,6 @@
         def _():
             for step in range(EARLY, 8):
                 send_first(1, step).start()
-
-        for block in (1, 3):
-
-            @pl.when((orbital == 1) & (me != OWNERS[block]))
-            def _(block=block):
-                send_back(0, 1, block, OWNERS[block]).start()
 
         for step in range(1, 8):
             source = tables.at[orbital, (me + 8 - step) % 8]
@@ -451,9 +444,7 @@
             lax.fori_loop(0, 16, turn, 0, unroll=2)
             for block, owner in enumerate(OWNERS):
 
-                later = (orbital == 0) & (part == 1) & (block % 2 == 1)
-
-                @pl.when((me != owner) & jnp.logical_not(later))
+                @pl.when(me != owner)
                 def _(block=block, owner=owner):
                     send_back(orbital, part, block, owner).start()
 

time: 172 us -> 162 us (0.942)
  Pallas kernels: 167 us -> 157 us
    pallas_call x1, Pallas kernels: 162 us -> 152 us  [line_of_chips(): pl.pallas_call(kernel, out_shape=jax.ShapeDtypeStruct((2, 128, 32, 128),...]
where the time goes in v7:
time: 162 us
  Pallas kernels  157 us (97%)
  local copies, waits for them, and re-layouts  2.39 us (1%)
  other arithmetic  1.73 us (1%)
    pallas_call x1, Pallas kernels, line_of_chips(): pl.pallas_call(kernel, out_shape=jax.ShapeDtypeStruct((2, 128, 32, 128),...  152 us
    pallas_call x1, Pallas kernels, pad(): pl.pallas_call(pad_kernel, out_shape=jax.ShapeDtypeStruct(shape, jnp.bflo...  5.03 us

profile of v7, /device:TPU:1, one launch (start us, length us, event | category | flops | bytes accessed | tf_op | source)
XLA Modules:
  0.0 162.1 jit_solution(4520209590868473157)
XLA Ops:
  0.7 1.7 %copy.11.own_proj = bf16[512,128]{1,0:T(8,128)(2,1)} copy(bf16[512,128]{0,1:T(8,128)(2,1)} %bitcast.5) | data formatting | bytes 262144 | tf_op jit(solution)/shard_map/reshape | solution.py:632
  2.3 1.1 multiply_convert_fusion
  3.4 0.6 pad_maximum_fusion
  4.1 0.7 copy.12.table_in
  4.8 152.2 %hamiltonian.1.value = bf16[2,128,32,128]{3,2,1,0:T(8,128)(2,1)} custom-call(s32[512]{0:T(512)} %cell.1, s32[1]{0:T(128)S(6)} %copy.13.count, f32[4]{0:T(128)} %dion.1, s32[1,512]{1,0:T(1,128)} %bitcast.6, s32[1,512]{1,0:T(1,128)} %bitcast.7, bf16[512,128]{1,0:T(8,128)(2,1)} %copy.11.own_proj, bf16[256,128]{1,0:T(8,128)(2,1)} %copy.12.table_in, ...), custom_call_target="tpu_custom_call" | custom-call | tf_op jit(solution)/shard_map/hamiltonian/pallas_call | solution.py:584
  157.0 5.0 %pad.9 = bf16[2,256,32,256]{3,2,1,0:T(8,128)(2,1)} custom-call(bf16[2,128,32,128]{3,2,1,0:T(8,128)(2,1)} %hamiltonian.1.value), custom_call_target="tpu_custom_call" | custom-call | tf_op jit(solution)/shard_map/pad/pallas_call | solution.py:561
  (1 shorter events, 0.0 us)
